TPU v7x, 32 devices: a whole 2x2x4 slice. The times are simulated.
32 devices in a mesh: req: 8 (over z, x), head: 4 (over y, core).
Axes of the slice: x: 2, y: 2, z: 4, core: 2. Of those that a mesh axis runs over, the one named last changes fastest.
Arguments:
- tokens: bfloat16 [384, 1024], P('req'), may hold values from -6 to 6
- cache_len: int32 [384], P('req'), may hold values from 1 to 1024, as said below
- page_table: int32 [384, 8], P('req'), may hold values from 0 to 159, as said below
- page_live: int32 [384, 8], P('req'), may hold values 0 or 1
- group_of: int32 [384], replicated, may hold values from 0 to 31, as said below
- kv_pool: bfloat16 [1280, 128, 2, 1024], P('req', None, None, 'head')
- enc_kv: bfloat16 [32, 2048, 2, 1024], P('req', None, None, 'head')
- w_self_in: bfloat16 [1024, 3, 1024], P('req', None, 'head'), may hold values from -0.1875 to 0.1875
- w_self_out: bfloat16 [1024, 1024], P('head', 'req'), may hold values from -0.75 to 0.75
- w_cross_q: bfloat16 [1024, 1024], P('req', 'head'), may hold values from -0.1875 to 0.1875
- w_cross_out: bfloat16 [1024, 1024], P('head', 'req'), may hold values from -0.75 to 0.75
- self_gain: float32 [1024], replicated, may hold values from 0.25 to 1.75
- self_bias: float32 [1024], replicated, may hold values from -1.75 to 1.75
- cross_gain: float32 [1024], replicated, may hold values from 0.25 to 1.75
- cross_bias: float32 [1024], replicated, may hold values from -1.75 to 1.75
Outputs:
- hidden_out: bfloat16 [384, 1024], P('req')
- new_kv: bfloat16 [384, 2, 1024], P('req', None, 'head')
Inputs may be any that keep to these rules, and one draw needn't show every extreme that they name: The pages of one device's requests, ceil(cache_len / 128) each, add up to at most 160; some request holds 1024 positions. `page_table`: for request r the slots j < ceil(cache_len[r] / 128) name pages of the pool part of r's index of req; no page is named by two such slots. Other slots hold any page number. `group_of`: every group has 8 to 16 requests; some group has exactly 16 and some exactly 8.
All inputs are finite; a program needn't handle non-finite values. No bound on the sum of `page_live` on one device may be relied on, other than what follows from the above.
Results may differ from a plain program's by a relative error of at most 0.019.
The roundings to bfloat16 on the way count: a program that leaves them out, or rounds other values in their place, can miss the bound.
Values may be sent and summed in bfloat16 or wider, within the bound.
A program may use at most 128 MiB of HBM per device.

v0:
```python
import jax
import jax.numpy as jnp
from jax import lax
from jax.sharding import PartitionSpec as P

HEAD_DIM = 64
GMAX = 16


def layer_norm(summed, gain_row, bias_row):
    center = summed - jnp.mean(summed, axis=-1, keepdims=True)
    spread = jnp.mean(center * center, axis=-1, keepdims=True)
    return center * lax.rsqrt(spread + 1e-05) * gain_row + bias_row


def head_total(partial_value):
    return lax.psum(partial_value, "head")


def paged_attention(query, new_key, new_value, cache_len, page_table, page_live, kv_pool, scale):
    pages_here, page_rows, _, head_cols = kv_pool.shape
    heads_here = head_cols // HEAD_DIM
    rows_here = query.shape[0]
    slots = page_table.shape[1]
    counts = (cache_len + page_rows - 1) // page_rows
    slot_index = jnp.arange(slots, dtype=jnp.int32)
    in_use = slot_index[None, :] < counts[:, None]
    hits = (
        page_table[:, :, None] == jnp.arange(pages_here, dtype=jnp.int32)[None, None, :]
    ) & in_use[:, :, None]
    owners = jnp.any(hits, axis=1)
    page_slot = jnp.sum(jnp.where(hits, slot_index[None, :, None], 0), axis=(0, 1))
    page_flag = jnp.sum(jnp.where(hits, page_live[:, :, None], 0), axis=(0, 1))
    page_length = jnp.sum(jnp.where(owners, cache_len[:, None], 0), axis=0)
    offsets = page_slot[:, None] * page_rows + jnp.arange(page_rows, dtype=jnp.int32)[None, :]
    counted = (page_flag[:, None] == 1) & (offsets < page_length[:, None])
    owner_weights = owners.astype(jnp.float32)
    page_query = jnp.dot(owners.T.astype(jnp.bfloat16), query, preferred_element_type=jnp.float32)
    page_query = page_query.astype(jnp.bfloat16).reshape(pages_here, heads_here, HEAD_DIM)
    stored = kv_pool.reshape(pages_here, page_rows, 2, heads_here, HEAD_DIM)
    scores = (
        jnp.einsum("pthd,phd->pht", stored[:, :, 0], page_query, preferred_element_type=jnp.float32)
        * scale
    )
    scores = jnp.where(counted[:, None, :], scores, -1e30)
    q_heads = query.astype(jnp.float32).reshape(rows_here, heads_here, HEAD_DIM)
    new_score = (
        jnp.sum(
            q_heads * new_key.astype(jnp.float32).reshape(rows_here, heads_here, HEAD_DIM), axis=-1
        )
        * scale
    )
    page_top = jnp.max(scores, axis=2)
    owner_top = jnp.max(jnp.where(owners[:, :, None], page_top[None, :, :], -1e30), axis=1)
    top = jnp.maximum(owner_top, new_score)
    page_shift = jnp.dot(owner_weights.T, top, precision=lax.Precision.HIGHEST)
    weights = jnp.where(counted[:, None, :], jnp.exp(scores - page_shift[:, :, None]), 0.0)
    new_weight = jnp.exp(new_score - top)
    total = (
        jnp.dot(owner_weights, jnp.sum(weights, axis=2), precision=lax.Precision.HIGHEST)
        + new_weight
    )
    page_sum = jnp.einsum(
        "pht,pthd->phd",
        weights.astype(jnp.bfloat16),
        stored[:, :, 1],
        preferred_element_type=jnp.float32,
    )
    summed = jnp.dot(
        owner_weights, page_sum.reshape(pages_here, head_cols), precision=lax.Precision.HIGHEST
    )
    rounded_new = lax.optimization_barrier(new_weight.astype(jnp.bfloat16)).astype(jnp.float32)
    own_term = rounded_new[:, :, None] * new_value.astype(jnp.float32).reshape(
        rows_here, heads_here, HEAD_DIM
    )
    summed = summed.reshape(rows_here, heads_here, HEAD_DIM) + own_term
    return (summed / total[:, :, None]).reshape(rows_here, head_cols).astype(jnp.bfloat16)


def group_attention(cross_query, group_of, enc_kv, scale):
    groups_here, positions, _, head_cols = enc_kv.shape
    heads_here = head_cols // HEAD_DIM
    every_query = lax.all_gather(cross_query, "req", axis=0, tiled=True)
    local_groups = lax.axis_index("req") * groups_here + jnp.arange(groups_here, dtype=jnp.int32)
    member = group_of[None, :] == local_groups[:, None]
    member_rank = jnp.cumsum(member.astype(jnp.int32), axis=1) - 1
    picker = member[:, None, :] & (
        member_rank[:, None, :] == jnp.arange(GMAX, dtype=jnp.int32)[None, :, None]
    )
    picker = picker.astype(jnp.bfloat16)
    group_query = jnp.einsum("gkr,rc->gkc", picker, every_query, preferred_element_type=jnp.float32)
    group_query = group_query.astype(jnp.bfloat16).reshape(groups_here, GMAX, heads_here, HEAD_DIM)
    stored = enc_kv.reshape(groups_here, positions, 2, heads_here, HEAD_DIM)
    scores = (
        jnp.einsum(
            "gehd,gkhd->gkhe", stored[:, :, 0], group_query, preferred_element_type=jnp.float32
        )
        * scale
    )
    top = jnp.max(scores, axis=3)
    weights = jnp.exp(scores - top[:, :, :, None])
    total = jnp.sum(weights, axis=3)
    summed = jnp.einsum(
        "gkhe,gehd->gkhd",
        weights.astype(jnp.bfloat16),
        stored[:, :, 1],
        preferred_element_type=jnp.float32,
    )
    context = (
        (summed / total[:, :, :, None]).astype(jnp.bfloat16).reshape(groups_here, GMAX, head_cols)
    )
    placed = jnp.einsum("gkr,gkc->rc", picker, context, preferred_element_type=jnp.float32)
    return lax.psum_scatter(placed.astype(jnp.bfloat16), "req", scatter_dimension=0, tiled=True)


def on_device(
    tokens,
    cache_len,
    page_table,
    page_live,
    group_of,
    kv_pool,
    enc_kv,
    w_self_in,
    w_self_out,
    w_cross_q,
    w_cross_out,
    self_gain,
    self_bias,
    cross_gain,
    cross_bias,
):
    rows_here = tokens.shape[0]
    width = tokens.shape[1]
    head_cols = kv_pool.shape[3]
    scale = HEAD_DIM ** (-0.5)
    full_in, full_out, full_query, full_cross = (
        lax.all_gather(w_self_in, "req", axis=0, tiled=True),
        lax.all_gather(w_self_out, "req", axis=1, tiled=True),
        lax.all_gather(w_cross_q, "req", axis=0, tiled=True),
        lax.all_gather(w_cross_out, "req", axis=1, tiled=True),
    )
    projected = jnp.dot(
        tokens, full_in.reshape(width, 3 * head_cols), preferred_element_type=jnp.float32
    )
    qkv = projected.astype(jnp.bfloat16).reshape(rows_here, 3, head_cols)
    self_ctx = paged_attention(
        qkv[:, 0], qkv[:, 1], qkv[:, 2], cache_len, page_table, page_live, kv_pool, scale
    )
    self_proj = head_total(jnp.dot(self_ctx, full_out, preferred_element_type=jnp.float32))
    h_first = layer_norm(tokens.astype(jnp.float32) + self_proj, self_gain, self_bias).astype(
        jnp.bfloat16
    )
    cross_query = jnp.dot(h_first, full_query, preferred_element_type=jnp.float32)
    cross_query = cross_query.astype(jnp.bfloat16)
    cross_ctx = group_attention(cross_query, group_of, enc_kv, scale)
    cross_proj = head_total(jnp.dot(cross_ctx, full_cross, preferred_element_type=jnp.float32))
    hidden_out = layer_norm(
        h_first.astype(jnp.float32) + cross_proj, cross_gain, cross_bias
    ).astype(jnp.bfloat16)
    return (hidden_out, qkv[:, 1:3])


def solution(mesh):
    return jax.shard_map(
        on_device,
        mesh=mesh,
        in_specs=(
            P("req", None),
            P("req"),
            P("req", None),
            P("req", None),
            P(),
            P("req", None, None, "head"),
            P("req", None, None, "head"),
            P("req", None, "head"),
            P("head", "req"),
            P("req", "head"),
            P("head", "req"),
            P(),
            P(),
            P(),
            P(),
        ),
        out_specs=(P("req", None), P("req", None, "head")),
        check_vma=False,
    )
```

profile of v0, /device:TPU:0, one launch (start us, length us, event | category | flops | bytes accessed | tf_op | source)
XLA Modules:
  0.0 321.1 jit_solution(16054848931703983183)
XLA Ops:
  7.2 1.8 copy.47
  9.0 0.8 copy.45
  9.8 0.8 copy.46
  10.6 50.0 %copy.49 = bf16[160,128,2,256]{1,3,2,0:T(8,128)(2,1)} copy(bf16[160,128,2,256]{3,2,1,0:T(2,128)(2,1)} %param.20) | data formatting | bytes 41943040 | tf_op args[5]
  60.7 1.2 reduce-window.6
  61.9 0.2 slice_reduce_fusion
  62.1 0.2 reduce-window.9
  62.4 0.2 fusion.17
  62.7 0.2 select_reduce_fusion.1
  63.1 0.1 fusion.29
  63.2 29.6 %all_gather.16 = bf16[256,1024]{1,0:T(8,128)(2,1)S(1)} all-gather(bf16[256,128]{1,0:T(8,128)(2,1)S(1)} %copy-done.2), channel_id=1, replica_groups=mesh['req'=8,'head'=4] {'req'}, dimensions={1}, use_global_device_ids=true | all-gather | bytes 589824 | tf_op jit(solution)/shard_map/all_gather | solution.py:139
  92.8 31.5 %all_gather.17 = bf16[1024,256]{1,0:T(8,128)(2,1)S(1)} all-gather(bf16[128,256]{1,0:T(8,128)(2,1)S(1)} %copy-done.3), channel_id=1, replica_groups=mesh['req'=8,'head'=4] {'req'}, dimensions={0}, use_global_device_ids=true | all-gather | bytes 589824 | tf_op jit(solution)/shard_map/all_gather | solution.py:140
  124.3 2.0 convolution_convert_fusion.1
  126.4 0.3 fusion.33
  126.7 0.2 convolution_convert_fusion
  127.0 0.2 copy.56
  127.2 5.5 %fusion.1 = f32[160,4,1,128]{3,2,1,0:T(1,128)S(1)} fusion(bf16[160,4,64,1]{2,3,1,0:T(2,128)(2,1)S(1)} %copy.56, bf16[160,128,2,4,64]{1,4,3,2,0:T(8,128)(2,1)} %bitcast.97), kind=kOutput, calls=%fused_computation.3 | convolution fusion | flops 10485760 | bytes 10895360 | tf_op jit(solution)/shard_map/pthd,phd->pht/dot_general | solution.py:42
  132.8 0.2 fusion.23
  133.2 0.1 reduce_sum.93
  133.4 0.1 fusion.43
  133.6 0.4 fusion.20
  134.0 0.1 convolution_add_fusion.1
  134.1 8.1 %fusion = f32[160,4,1,64]{3,2,1,0:T(1,128)S(1)} fusion(bf16[160,128,2,4,64]{1,4,3,2,0:T(8,128)(2,1)} %bitcast.98, bf16[160,4,128,1]{2,0,1,3:T(8,128)(2,1)S(1)} %get-tuple-element.7), kind=kOutput, calls=%fused_computation.1 | convolution fusion | flops 10485760 | bytes 10813440 | tf_op jit(solution)/shard_map/pht,pthd->phd/dot_general | solution.py:63
  142.2 0.2 copy.59
  142.5 0.3 fusion.11
  143.0 0.9 fusion.50
  144.0 21.3 %copy.53 = bf16[4,2048,2,256]{1,3,0,2:T(8,128)(2,1)} copy(bf16[4,2048,2,256]{3,2,1,0:T(2,128)(2,1)} %param.21) | data formatting | bytes 16777216 | tf_op args[6]
  165.4 9.6 %all-reduce.3.cloned.1.call-done = f32[48,1024]{1,0:T(8,128)} async-done(((f32[48,1024]{1,0:T(8,128)}), f32[48,1024]{1,0:T(8,128)}) %all-reduce.3.cloned.1.call-update) | async-done | bytes 196624 | tf_op jit(solution)/shard_map/psum | solution.py:17
  174.9 1.1 fusion.30
  176.0 1.1 multiply_reduce_fusion.1
  177.2 1.0 add_convert_fusion.1
  178.2 0.2 convolution_convert_fusion.3
  178.4 30.8 %all_gather.18 = bf16[384,256]{1,0:T(8,128)(2,1)S(1)} all-gather(bf16[48,256]{1,0:T(8,128)(2,1)S(1)} %convolution_convert_fusion.3), channel_id=1, replica_groups=mesh['req'=8,'head'=4] {'req'}, dimensions={0}, use_global_device_ids=true | all-gather | bytes 221184 | tf_op jit(solution)/shard_map/all_gather | solution.py:83
  209.2 0.2 convolution_convert_fusion.2
  209.4 3.1 fusion.49
  212.5 0.4 fusion.6
  213.0 1.1 copy-done
  214.1 1.3 fusion.13
  215.4 0.1 reshape.215
  215.5 0.9 fusion.8
  216.5 27.8 %all_gather.19 = bf16[256,1024]{1,0:T(8,128)(2,1)S(1)} all-gather(bf16[256,128]{1,0:T(8,128)(2,1)S(1)} %copy-done.4), channel_id=1, replica_groups=mesh['req'=8,'head'=4] {'req'}, dimensions={1}, use_global_device_ids=true | all-gather | bytes 589824 | tf_op jit(solution)/shard_map/all_gather | solution.py:141
  244.3 33.3 %reduce-scatter.2.cloned.1.call-done = bf16[48,256]{1,0:T(8,128)(2,1)} async-done(((bf16[384,256]{1,0:T(8,128)(2,1)}), bf16[48,256]{1,0:T(8,128)(2,1)}) %reduce-scatter.2.cloned.1.call-update) | async-done | bytes 24592 | tf_op jit(solution)/shard_map/reduce_scatter | solution.py:113
  277.6 1.6 fusion.51
  279.2 0.7 slice.48
  279.9 30.8 %all-reduce.5.cloned.1.call-done = f32[48,1024]{1,0:T(8,128)} async-done(((f32[48,1024]{1,0:T(8,128)}), f32[48,1024]{1,0:T(8,128)}) %all-reduce.5.cloned.1.call-update) | async-done | bytes 196624 | tf_op jit(solution)/shard_map/psum | solution.py:17
  310.7 1.1 fusion.31
  311.7 1.1 multiply_reduce_fusion
  312.9 1.7 add_convert_fusion
  (57 shorter events, 1.6 us)
Async XLA Ops:
  7.2 117.1 %all-gather.2.cloned.1.call-start = ((), (), s32[]{:S(2)}) async-start(), calls=%async_computation.1 | async-start | bytes 1769472 | tf_op jit(solution)/shard_map/all_gather | solution.py:138
  9.0 165.9 %all-reduce.3.cloned.1.call-start = ((), (), s32[]{:S(2)}) async-start(), calls=%async_computation.2 | async-start | bytes 393216 | tf_op jit(solution)/shard_map/psum | solution.py:17
  10.6 50.1 %copy-start.5 = (s32[384]{0:T(512)S(1)}, s32[384]{0:T(512)}, u32[]{:S(2)}) copy-start(s32[384]{0:T(512)} %param.19) | copy-start | bytes 4612
  10.6 51.8 %copy-start.10 = (s32[48]{0:T(128)S(1)}, s32[48]{0:T(128)}, u32[]{:S(2)}) copy-start(s32[48]{0:T(128)} %param.16) | copy-start | bytes 580
  10.6 52.6 %copy-start.2 = (bf16[256,128]{1,0:T(8,128)(2,1)S(1)}, bf16[256,128]{1,0:T(8,128)(2,1)}, u32[]{:S(2)}) copy-start(bf16[256,128]{1,0:T(8,128)(2,1)} %param.23) | copy-start | bytes 196612
  10.6 82.2 %copy-start.3 = (bf16[128,256]{1,0:T(8,128)(2,1)S(1)}, bf16[128,256]{1,0:T(8,128)(2,1)}, u32[]{:S(2)}) copy-start(bf16[128,256]{1,0:T(8,128)(2,1)} %param.24) | copy-start | bytes 196612
  10.6 113.7 %copy-start.1 = (bf16[48,1024]{1,0:T(8,128)(2,1)S(1)}, bf16[48,1024]{1,0:T(8,128)(2,1)}, u32[]{:S(2)}) copy-start(bf16[48,1024]{1,0:T(8,128)(2,1)} %param.15) | copy-start | bytes 294916
  143.9 133.7 %reduce-scatter.2.cloned.1.call-start = ((), (), s32[]{:S(2)}) async-start(), calls=%async_computation.3 | async-start | bytes 221184 | tf_op jit(solution)/shard_map/reduce_scatter | solution.py:113
  144.0 33.1 %copy-start.6 = (f32[1024]{0:T(1024)S(1)}, f32[1024]{0:T(1024)}, u32[]{:S(2)}) copy-start(f32[1024]{0:T(1024)} %param.27) | copy-start | bytes 12292
  144.0 33.1 %copy-start.7 = (f32[1024]{0:T(1024)S(1)}, f32[1024]{0:T(1024)}, u32[]{:S(2)}) copy-start(f32[1024]{0:T(1024)} %param.26) | copy-start | bytes 12292
  209.4 4.6 %copy-start = (bf16[4,2048,2,256]{1,3,0,2:T(8,128)(2,1)S(1)}, bf16[4,2048,2,256]{1,3,0,2:T(8,128)(2,1)}, u32[]{:S(2)}) copy-start(bf16[4,2048,2,256]{1,3,0,2:T(8,128)(2,1)} %copy.53) | copy-start | bytes 25165828
  214.1 2.4 copy-start.4
  214.1 98.8 %copy-start.8 = (f32[1024]{0:T(1024)S(1)}, f32[1024]{0:T(1024)}, u32[]{:S(2)}) copy-start(f32[1024]{0:T(1024)} %param.29) | copy-start | bytes 12292
  214.1 98.8 %copy-start.9 = (f32[1024]{0:T(1024)S(1)}, f32[1024]{0:T(1024)}, u32[]{:S(2)}) copy-start(f32[1024]{0:T(1024)} %param.28) | copy-start | bytes 12292
  216.5 94.2 %all-reduce.5.cloned.1.call-start = ((), (), s32[]{:S(2)}) async-start(), calls=%async_computation.4 | async-start | bytes 393216 | tf_op jit(solution)/shard_map/psum | solution.py:17
Sparse Core Ops, SparseCore 0:
  10.0 47.9 all-gather.1
  144.0 30.8 all-reduce.2
  216.6 60.9 reduce-scatter.1
  279.9 30.7 all-reduce.4
where the time goes:
time: 323 us; the launch traced here: 321 us
  blocking collectives  120 us (37%)
  local copies, waits for them, and re-layouts  77.9 us (24%)
  waiting for transfers between devices  73.7 us (23%)
  matrix products  24.6 us (8%)
  between operations  14 us (4%)
  other arithmetic  11.1 us (3%)
    unnamed x28, local copies, waits for them, and re-layouts  75.8 us
    psum x2, waiting for transfers between devices, head_total(): return lax.psum(partial_value, 'head')  40.3 us
    reduce_scatter x1, waiting for transfers between devices, group_attention(): lax.psum_scatter(placed.astype(jnp.bfloat16), 'req', scatter_dimension=0,...  33.3 us
    all_gather x1, blocking collectives, on_device(): lax.all_gather(w_cross_q, 'req', axis=0, tiled=True)  31.5 us
    all_gather x1, blocking collectives, group_attention(): every_query = lax.all_gather(cross_query, 'req', axis=0, tiled=True)  30.8 us
    all_gather x1, blocking collectives, on_device(): lax.all_gather(w_self_out, 'req', axis=1, tiled=True)  29.6 us
    all_gather x1, blocking collectives, on_device(): lax.all_gather(w_cross_out, 'req', axis=1, tiled=True)  27.8 us
    dot_general x1, matrix products, paged_attention(): jnp.einsum('pht,pthd->phd', weights.astype(jnp.bfloat16), stored[:, :, 1]...  8.12 us
  transfers between devices with their start and end apart: 4, of which 3 were waited for; matrix products, arithmetic and copies ran while one was open for 24% of the time, Pallas kernels for 0%

commit v1 on v0

v1 whole, which is shorter than its diff:
```python
import functools

import jax
import jax.numpy as jnp
from jax import lax
from jax.experimental import pallas as pl
from jax.experimental.pallas import tpu as pltpu
from jax.sharding import PartitionSpec as P

HEAD_DIM = 64
GMAX = 16


def layer_norm(summed, gain_row, bias_row):
    center = summed - jnp.mean(summed, axis=-1, keepdims=True)
    spread = jnp.mean(center * center, axis=-1, keepdims=True)
    return center * lax.rsqrt(spread + 1e-05) * gain_row + bias_row


def head_total(partial_value):
    return lax.psum(partial_value, "head")


LANES = 128
NEG = -1e30
VMEM_LIMIT = 60 * 1024 * 1024


def pair_copies(source, rows, start, held, sems, slot):
    return [
        pltpu.make_async_copy(
            source.at[pl.ds(start, rows), pl.ds(half * LANES, LANES)],
            held.at[slot, half],
            sems.at[slot, half],
        )
        for half in range(held.shape[1])
    ]


def page_kernel(valid_ref, query_ref, kv_ref, acc_ref, top_ref, total_ref, held, sems, *, batch):
    pages, page_rows, _, cols = kv_ref.shape
    heads = cols // HEAD_DIM
    span = 2 * page_rows
    source = kv_ref.reshape(pages * span, cols)
    steps = pages // batch
    rows = batch * span
    slots = held.shape[0]
    for step in range(min(slots, steps)):
        for copy in pair_copies(source, rows, step * rows, held, sems, step):
            copy.start()
    head_row = lax.broadcasted_iota(jnp.int32, (8, cols), 0)
    head_mask = head_row == lax.broadcasted_iota(jnp.int32, (8, cols), 1) // HEAD_DIM
    column = lax.broadcasted_iota(jnp.int32, (8, span), 1)
    is_key = column % 2 == 0

    def body(step, carry):
        slot = lax.rem(step, slots)
        for copy in pair_copies(source, rows, step * rows, held, sems, slot):
            copy.wait()
        accs, tops, totals = [], [], []
        for page in range(batch):
            valid = valid_ref[step * batch + page]
            states = jnp.concatenate(
                [held[slot, half, pl.ds(page * span, span), :] for half in range(held.shape[1])], axis=1
            )
            query = query_ref[pl.ds(step * batch + page, 1), :]
            spread = jnp.where(head_mask, jnp.broadcast_to(query, (8, cols)), 0.0).astype(jnp.bfloat16)
            scores = lax.dot_general(
                spread, states, (((1,), (1,)), ((), ())), preferred_element_type=jnp.float32
            )
            counted = is_key & (column < 2 * valid)
            scores = jnp.where(counted, scores, NEG)
            top = jnp.max(scores, axis=1, keepdims=True)
            weights = jnp.where(counted, jnp.exp(scores - top), 0.0)
            total = jnp.sum(weights, axis=1, keepdims=True)
            moved = pltpu.roll(weights, 1, 1).astype(jnp.bfloat16)
            summed = jnp.dot(moved, states, preferred_element_type=jnp.float32)
            accs.append(jnp.sum(jnp.where(head_mask, summed, 0.0), axis=0, keepdims=True))
            tops.append(jnp.sum(jnp.where(head_mask, top, 0.0), axis=0, keepdims=True))
            totals.append(jnp.sum(jnp.where(head_mask, total, 0.0), axis=0, keepdims=True))
        here = pl.ds(pl.multiple_of(step * batch, batch), batch)
        acc_ref[here, :] = jnp.concatenate(accs, axis=0)
        top_ref[here, :] = jnp.concatenate(tops, axis=0)
        total_ref[here, :] = jnp.concatenate(totals, axis=0)

        @pl.when(step + slots < steps)
        def _():
            for copy in pair_copies(source, rows, (step + slots) * rows, held, sems, slot):
                copy.start()

        return carry

    lax.fori_loop(0, steps, body, 0)


def page_parts(page_valid, page_query, kv_pool):
    pages, page_rows, _, cols = kv_pool.shape
    batch = 8
    slots = min(8, pages // batch)
    part = jax.ShapeDtypeStruct((pages, cols), jnp.float32)
    return pl.pallas_call(
        functools.partial(page_kernel, batch=batch),
        out_shape=(part, part, part),
        in_specs=[
            pl.BlockSpec(memory_space=pltpu.SMEM),
            pl.BlockSpec(memory_space=pltpu.VMEM),
            pl.BlockSpec(memory_space=pl.ANY),
        ],
        out_specs=(pl.BlockSpec(memory_space=pltpu.VMEM),) * 3,
        scratch_shapes=[
            pltpu.VMEM((slots, cols // LANES, batch * 2 * page_rows, LANES), jnp.bfloat16),
            pltpu.SemaphoreType.DMA((slots, cols // LANES)),
        ],
        compiler_params=pltpu.CompilerParams(vmem_limit_bytes=VMEM_LIMIT),
        cost_estimate=pl.CostEstimate(
            flops=pages * 8 * 2 * page_rows * cols * 4,
            bytes_accessed=pages * page_rows * 4 * cols,
            transcendentals=pages * 16 * page_rows,
        ),
        name="page_parts",
    )(page_valid, page_query, kv_pool)


def paged_attention(query, new_key, new_value, cache_len, page_table, page_live, kv_pool, scale):
    pages_here, page_rows, _, head_cols = kv_pool.shape
    heads_here = head_cols // HEAD_DIM
    rows_here = query.shape[0]
    slots = page_table.shape[1]
    counts = (cache_len + page_rows - 1) // page_rows
    slot_index = jnp.arange(slots, dtype=jnp.int32)
    in_use = slot_index[None, :] < counts[:, None]
    hits = (
        page_table[:, :, None] == jnp.arange(pages_here, dtype=jnp.int32)[None, None, :]
    ) & in_use[:, :, None]
    owners = jnp.any(hits, axis=1)
    slot_valid = jnp.where(
        page_live == 1,
        jnp.clip(cache_len[:, None] - slot_index[None, :] * page_rows, 0, page_rows),
        0,
    )
    page_valid = jnp.sum(jnp.where(hits, slot_valid[:, :, None], 0), axis=(0, 1))
    owner_weights = owners.astype(jnp.float32)
    scaled = (query * scale).astype(jnp.bfloat16)
    page_query = jnp.dot(owners.T.astype(jnp.bfloat16), scaled, preferred_element_type=jnp.float32)
    page_sum, page_top, page_total = page_parts(page_valid, page_query, kv_pool)
    products = query.astype(jnp.float32) * new_key.astype(jnp.float32)
    new_score = jnp.sum(products.reshape(rows_here, heads_here, HEAD_DIM), axis=-1) * scale
    new_score = jnp.repeat(new_score, HEAD_DIM, axis=1)
    counted = owners & (page_valid > 0)[None, :]
    owner_top = jnp.max(jnp.where(counted[:, :, None], page_top[None, :, :], NEG), axis=1)
    top = jnp.maximum(owner_top, new_score)
    page_shift = jnp.dot(owner_weights.T, top, precision=lax.Precision.HIGHEST)
    factor = jnp.where((page_valid > 0)[:, None], jnp.exp(page_top - page_shift), 0.0)
    new_weight = jnp.exp(new_score - top)
    both = jnp.dot(
        owner_weights,
        jnp.concatenate([page_sum * factor, page_total * factor], axis=1),
        precision=lax.Precision.HIGHEST,
    )
    rounded_new = lax.optimization_barrier(new_weight.astype(jnp.bfloat16)).astype(jnp.float32)
    summed = both[:, :head_cols] + rounded_new * new_value.astype(jnp.float32)
    return (summed / (both[:, head_cols:] + new_weight)).astype(jnp.bfloat16)


def group_kernel(picker_ref, query_ref, kv_ref, out_ref, held, scores_ref, sems):
    groups, positions, _, cols = kv_ref.shape
    heads = cols // HEAD_DIM
    span = 2 * positions
    source = kv_ref.reshape(groups * span, cols)
    for group in range(groups):
        for copy in pair_copies(source, span, group * span, held, sems, group):
            copy.start()
    lane_head = lax.broadcasted_iota(jnp.int32, (GMAX, cols), 1) // HEAD_DIM
    block = min(512, span)
    is_key = lax.broadcasted_iota(jnp.int32, (heads * GMAX, block), 1) % 2 == 0
    placed = jnp.zeros(out_ref.shape, jnp.float32)
    for group in range(groups):
        picker = picker_ref[pl.ds(group * GMAX, GMAX), :]
        query = jnp.dot(picker, query_ref[...], preferred_element_type=jnp.float32)
        spread = jnp.concatenate(
            [jnp.where(lane_head == head, query, 0.0) for head in range(heads)], axis=0
        ).astype(jnp.bfloat16)
        for copy in pair_copies(source, span, group * span, held, sems, group):
            copy.wait()

        def states_of(at):
            return jnp.concatenate(
                [held[group, half, pl.ds(at, block), :] for half in range(held.shape[1])], axis=1
            )

        top = jnp.full((heads * GMAX, 1), NEG, jnp.float32)
        for at in range(0, span, block):
            scores = lax.dot_general(
                spread, states_of(at), (((1,), (1,)), ((), ())), preferred_element_type=jnp.float32
            )
            scores = jnp.where(is_key, scores, NEG)
            scores_ref[:, pl.ds(at, block)] = scores
            top = jnp.maximum(top, jnp.max(scores, axis=1, keepdims=True))
        total = jnp.zeros((heads * GMAX, 1), jnp.float32)
        summed = jnp.zeros((heads * GMAX, cols), jnp.float32)
        for at in range(0, span, block):
            weights = jnp.where(is_key, jnp.exp(scores_ref[:, pl.ds(at, block)] - top), 0.0)
            total += jnp.sum(weights, axis=1, keepdims=True)
            moved = pltpu.roll(weights, 1, 1).astype(jnp.bfloat16)
            summed += jnp.dot(moved, states_of(at), preferred_element_type=jnp.float32)
        summed = summed / total
        context = jnp.zeros((GMAX, cols), jnp.float32)
        for head in range(heads):
            context += jnp.where(lane_head == head, summed[head * GMAX : (head + 1) * GMAX], 0.0)
        placed += lax.dot_general(
            picker,
            context.astype(jnp.bfloat16),
            (((0,), (0,)), ((), ())),
            preferred_element_type=jnp.float32,
        )
    out_ref[...] = placed.astype(jnp.bfloat16)


def group_parts(picker, queries, enc_kv):
    groups, positions, _, cols = enc_kv.shape
    heads = cols // HEAD_DIM
    return pl.pallas_call(
        group_kernel,
        out_shape=jax.ShapeDtypeStruct(queries.shape, jnp.bfloat16),
        in_specs=[
            pl.BlockSpec(memory_space=pltpu.VMEM),
            pl.BlockSpec(memory_space=pltpu.VMEM),
            pl.BlockSpec(memory_space=pl.ANY),
        ],
        out_specs=pl.BlockSpec(memory_space=pltpu.VMEM),
        scratch_shapes=[
            pltpu.VMEM((groups, cols // LANES, 2 * positions, LANES), jnp.bfloat16),
            pltpu.VMEM((heads * GMAX, 2 * positions), jnp.float32),
            pltpu.SemaphoreType.DMA((groups, cols // LANES)),
        ],
        compiler_params=pltpu.CompilerParams(vmem_limit_bytes=VMEM_LIMIT),
        name="group_parts",
    )(picker, queries, enc_kv)


def group_picker(group_of, groups_here):
    local_groups = lax.axis_index("req") * groups_here + jnp.arange(groups_here, dtype=jnp.int32)
    member = group_of[None, :] == local_groups[:, None]
    member_rank = jnp.cumsum(member.astype(jnp.int32), axis=1) - 1
    picker = member[:, None, :] & (
        member_rank[:, None, :] == jnp.arange(GMAX, dtype=jnp.int32)[None, :, None]
    )
    return picker.astype(jnp.bfloat16).reshape(groups_here * GMAX, -1)


def group_attention(cross_query, group_of, enc_kv, scale):
    scaled = (cross_query * scale).astype(jnp.bfloat16)
    every_query = lax.all_gather(scaled, "req", axis=0, tiled=True)
    picker = group_picker(group_of, enc_kv.shape[0])
    placed = group_parts(picker, every_query, enc_kv)
    return lax.psum_scatter(placed, "req", scatter_dimension=0, tiled=True)


def on_device(
    tokens,
    cache_len,
    page_table,
    page_live,
    group_of,
    kv_pool,
    enc_kv,
    w_self_in,
    w_self_out,
    w_cross_q,
    w_cross_out,
    self_gain,
    self_bias,
    cross_gain,
    cross_bias,
):
    rows_here = tokens.shape[0]
    width = tokens.shape[1]
    head_cols = kv_pool.shape[3]
    scale = HEAD_DIM ** (-0.5)
    full_in, full_out, full_query, full_cross = (
        lax.all_gather(w_self_in, "req", axis=0, tiled=True),
        lax.all_gather(w_self_out, "req", axis=1, tiled=True),
        lax.all_gather(w_cross_q, "req", axis=0, tiled=True),
        lax.all_gather(w_cross_out, "req", axis=1, tiled=True),
    )
    projected = jnp.dot(
        tokens, full_in.reshape(width, 3 * head_cols), preferred_element_type=jnp.float32
    )
    qkv = projected.astype(jnp.bfloat16).reshape(rows_here, 3, head_cols)
    self_ctx = paged_attention(
        qkv[:, 0], qkv[:, 1], qkv[:, 2], cache_len, page_table, page_live, kv_pool, scale
    )
    self_proj = head_total(jnp.dot(self_ctx, full_out, preferred_element_type=jnp.float32))
    h_first = layer_norm(tokens.astype(jnp.float32) + self_proj, self_gain, self_bias).astype(
        jnp.bfloat16
    )
    cross_query = jnp.dot(h_first, full_query, preferred_element_type=jnp.float32)
    cross_query = cross_query.astype(jnp.bfloat16)
    cross_ctx = group_attention(cross_query, group_of, enc_kv, scale)
    cross_proj = head_total(jnp.dot(cross_ctx, full_cross, preferred_element_type=jnp.float32))
    hidden_out = layer_norm(
        h_first.astype(jnp.float32) + cross_proj, cross_gain, cross_bias
    ).astype(jnp.bfloat16)
    return (hidden_out, qkv[:, 1:3])


def solution(mesh):
    return jax.shard_map(
        on_device,
        mesh=mesh,
        in_specs=(
            P("req", None),
            P("req"),
            P("req", None),
            P("req", None),
            P(),
            P("req", None, None, "head"),
            P("req", None, None, "head"),
            P("req", None, "head"),
            P("head", "req"),
            P("req", "head"),
            P("head", "req"),
            P(),
            P(),
            P(),
            P(),
        ),
        out_specs=(P("req", None), P("req", None, "head")),
        check_vma=False,
    )
```

time: 323 us -> 331 us (1.025)
  local copies, waits for them, and re-layouts: 77.9 us -> 3.98 us
  Pallas kernels: 0 us -> 71 us
  waiting for transfers between devices: 73.7 us -> 93.5 us
  matrix products: 24.6 us -> 7.27 us
  other arithmetic: 11.1 us -> 16.2 us
  blocking collectives: 120 us -> 124 us
    unnamed x28 -> x19, local copies, waits for them, and re-layouts: 75.8 us -> 2.55 us
    pallas_call x0 -> x2, Pallas kernels: none -> 71 us  [the longest x1 59.5 us: page_parts(): pl.pallas_call(functools.partial(page_kernel, batch=batch), out_shape=(pa...]
    psum x2, waiting for transfers between devices: 40.3 us -> 60.1 us  [head_total(): return lax.psum(partial_value, 'head')]
    dot_general x9 -> x2, matrix products: 19.8 us -> 1.13 us  [the longest x1 0.88 us: paged_attention(): jnp.dot(owners.T.astype(jnp.bfloat16), scaled, preferred_element_type=jnp...]
  transfers between devices with their start and end apart: 4 -> 4, of which waited for: 3 -> 3; matrix products, arithmetic and copies ran while one was open for 24% -> 2% of each run, Pallas kernels for 0% -> 0%
where the time goes in v1:
time: 331 us; the launch traced here: 330 us
  blocking collectives  124 us (37%)
  waiting for transfers between devices  93.5 us (28%)
  Pallas kernels  71 us (21%)
  other arithmetic  16.2 us (5%)
  between operations  14 us (4%)
  matrix products  7.27 us (2%)
  local copies, waits for them, and re-layouts  3.98 us (1%)
    psum x2, waiting for transfers between devices, head_total(): return lax.psum(partial_value, 'head')  60.1 us
    pallas_call x1, Pallas kernels, page_parts(): pl.pallas_call(functools.partial(page_kernel, batch=batch), out_shape=(pa...  59.5 us
    reduce_scatter x1, waiting for transfers between devices, group_attention(): return lax.psum_scatter(placed, 'req', scatter_dimension=0, tiled=True)  33.3 us
    all_gather x1, blocking collectives, on_device(): lax.all_gather(w_cross_q, 'req', axis=0, tiled=True)  32.8 us
    all_gather x1, blocking collectives, group_attention(): every_query = lax.all_gather(scaled, 'req', axis=0, tiled=True)  32.7 us
    all_gather x1, blocking collectives, on_device(): lax.all_gather(w_self_out, 'req', axis=1, tiled=True)  31 us
    all_gather x1, blocking collectives, on_device(): lax.all_gather(w_cross_out, 'req', axis=1, tiled=True)  27.8 us
    pallas_call x1, Pallas kernels, group_parts(): pl.pallas_call(group_kernel, out_shape=jax.ShapeDtypeStruct(queries.shape...  11.5 us
  transfers between devices with their start and end apart: 4, of which 3 were waited for; matrix products, arithmetic and copies ran while one was open for 2% of the time, Pallas kernels for 0%

profile of v1, /device:TPU:0, one launch (start us, length us, event | category | flops | bytes accessed | tf_op | source)
XLA Modules:
  0.0 330.4 jit_solution(13574388788928517796)
XLA Ops:
  7.2 1.7 copy.26
  9.0 0.8 copy.24
  9.8 0.8 clamp_select_fusion
  10.6 0.1 copy.25
  10.6 0.8 compare_convert_fusion
  11.4 1.2 reduce-window.6
  12.6 0.2 slice_reduce_fusion
  12.8 0.2 reduce-window.9
  13.0 0.7 and_select_fusion
  13.7 0.1 iota_compare_fusion.1
  13.7 0.2 fusion.4
  14.0 0.2 select_reduce_fusion.1.valid_ref
  14.2 0.1 add_bitcast_fusion
  14.3 31.0 %all_gather.16 = bf16[256,1024]{1,0:T(8,128)(2,1)S(1)} all-gather(bf16[256,128]{1,0:T(8,128)(2,1)} %param.23), channel_id=1, replica_groups=mesh['req'=8,'head'=4] {'req'}, dimensions={1}, use_global_device_ids=true | all-gather | bytes 589824 | tf_op jit(solution)/shard_map/all_gather | solution.py:282
  45.3 32.8 %all_gather.17 = bf16[1024,256]{1,0:T(8,128)(2,1)S(1)} all-gather(bf16[128,256]{1,0:T(8,128)(2,1)} %param.24), channel_id=1, replica_groups=mesh['req'=8,'head'=4] {'req'}, dimensions={0}, use_global_device_ids=true | all-gather | bytes 589824 | tf_op jit(solution)/shard_map/all_gather | solution.py:283
  78.1 2.1 convolution_convert_fusion
  80.2 0.1 fusion.26
  80.3 0.2 fusion.16
  80.5 0.9 fusion.20.query_ref
  81.4 0.1 mul.88
  81.5 0.1 reduce_sum.55
  81.6 0.1 broadcast_in_dim.54
  81.7 0.1 reshape.164
  81.9 59.5 %page_parts.1 = (f32[160,256]{1,0:T(8,128)}, f32[160,256]{1,0:T(8,128)}, f32[160,256]{1,0:T(8,128)}) custom-call(s32[160]{0:T(256)} %copy-done.7, f32[160,256]{1,0:T(8,128)} %fusion.20.query_ref, bf16[160,128,2,256]{3,2,1,0:T(2,128)(2,1)} %kv_ref.2), custom_call_target="tpu_custom_call" | custom-call | flops 335544320 | bytes 20971520 | tf_op jit(solution)/shard_map/page_parts/pallas_call | solution.py:101
  141.5 3.6 %select_reduce_fusion = f32[48,256]{1,0:T(8,128)S(1)} fusion(f32[160,256]{1,0:T(8,128)} %get-tuple-element.6, pred[48,160]{1,0:T(8,128)(4,1)S(1)} %broadcast_and_fusion), kind=kLoop, calls=%fused_computation | loop fusion | flops 3919872 | bytes 220672 | tf_op jit(solution)/shard_map/reduce_max | solution.py:150
  145.2 1.4 fusion.25
  146.5 0.3 fusion.5
  146.8 0.9 fusion.18
  147.7 0.0 reduce-scatter.2.cloned.1.call-start
  147.8 0.1 broadcast_compare_fusion
  147.9 0.1 eq.80
  147.9 0.7 fusion.10.picker_ref
  148.7 29.4 %all-reduce.3.cloned.1.call-done = f32[48,1024]{1,0:T(8,128)} async-done(((f32[48,1024]{1,0:T(8,128)}), f32[48,1024]{1,0:T(8,128)}) %all-reduce.3.cloned.1.call-update) | async-done | bytes 196624 | tf_op jit(solution)/shard_map/psum | solution.py:21
  178.0 1.1 fusion.11
  179.1 1.1 multiply_reduce_fusion.1
  180.3 1.0 add_convert_fusion.1
  181.3 0.2 fusion.2
  181.5 32.7 %all_gather.18.query_ref = bf16[384,256]{1,0:T(8,128)(2,1)} all-gather(bf16[48,256]{1,0:T(8,128)(2,1)S(1)} %fusion.2), channel_id=1, replica_groups=mesh['req'=8,'head'=4] {'req'}, dimensions={0}, use_global_device_ids=true | all-gather | bytes 221184 | tf_op jit(solution)/shard_map/all_gather | solution.py:253
  214.2 11.5 %group_parts.1 = bf16[384,256]{1,0:T(8,128)(2,1)} custom-call(bf16[64,384]{1,0:T(8,128)(2,1)} %fusion.10.picker_ref, bf16[384,256]{1,0:T(8,128)(2,1)} %all_gather.18.query_ref, bf16[4,2048,2,256]{3,2,1,0:T(2,128)(2,1)} %kv_ref.3), custom_call_target="tpu_custom_call" | custom-call | tf_op jit(solution)/shard_map/group_parts/pallas_call | solution.py:222
  225.7 0.0 all-reduce.5.cloned.1.call-start
  225.8 27.8 %all_gather.19 = bf16[256,1024]{1,0:T(8,128)(2,1)S(1)} all-gather(bf16[256,128]{1,0:T(8,128)(2,1)S(1)} %copy-done.1), channel_id=1, replica_groups=mesh['req'=8,'head'=4] {'req'}, dimensions={1}, use_global_device_ids=true | all-gather | bytes 589824 | tf_op jit(solution)/shard_map/all_gather | solution.py:284
  253.6 33.3 %reduce-scatter.2.cloned.1.call-done = bf16[48,256]{1,0:T(8,128)(2,1)} async-done(((bf16[384,256]{1,0:T(8,128)(2,1)}), bf16[48,256]{1,0:T(8,128)(2,1)}) %reduce-scatter.2.cloned.1.call-update) | async-done | bytes 24592 | tf_op jit(solution)/shard_map/reduce_scatter | solution.py:256
  286.9 1.6 fusion.27
  288.5 0.7 slice.38
  289.2 30.7 %all-reduce.5.cloned.1.call-done = f32[48,1024]{1,0:T(8,128)} async-done(((f32[48,1024]{1,0:T(8,128)}), f32[48,1024]{1,0:T(8,128)}) %all-reduce.5.cloned.1.call-update) | async-done | bytes 196624 | tf_op jit(solution)/shard_map/psum | solution.py:21
  320.0 1.1 fusion.12
  321.0 1.1 multiply_reduce_fusion
  322.2 1.7 add_convert_fusion
  (36 shorter events, 0.3 us)
Async XLA Ops:
  7.2 70.9 %all-gather.2.cloned.1.call-start = ((), (), s32[]{:S(2)}) async-start(), calls=%async_computation.1 | async-start | bytes 1769472 | tf_op jit(solution)/shard_map/all_gather | solution.py:281
  9.0 169.1 %all-reduce.3.cloned.1.call-start = ((), (), s32[]{:S(2)}) async-start(), calls=%async_computation.2 | async-start | bytes 393216 | tf_op jit(solution)/shard_map/psum | solution.py:21
  14.2 67.6 %copy-start.7 = (s32[160]{0:T(256)}, s32[160]{0:T(256)S(1)}, u32[]{:S(2)}) copy-start(s32[160]{0:T(256)S(1)} %select_reduce_fusion.1.valid_ref) | copy-start | bytes 1924
  81.9 65.9 %copy-start.2 = (s32[384]{0:T(512)S(1)}, s32[384]{0:T(512)}, u32[]{:S(2)}) copy-start(s32[384]{0:T(512)} %param.19) | copy-start | bytes 4612
  81.9 96.2 %copy-start = (bf16[48,1024]{1,0:T(8,128)(2,1)S(1)}, bf16[48,1024]{1,0:T(8,128)(2,1)}, u32[]{:S(2)}) copy-start(bf16[48,1024]{1,0:T(8,128)(2,1)} %param.15) | copy-start | bytes 294916
  81.9 98.4 %copy-start.3 = (f32[1024]{0:T(1024)S(1)}, f32[1024]{0:T(1024)}, u32[]{:S(2)}) copy-start(f32[1024]{0:T(1024)} %param.27) | copy-start | bytes 12292
  81.9 98.4 %copy-start.4 = (f32[1024]{0:T(1024)S(1)}, f32[1024]{0:T(1024)}, u32[]{:S(2)}) copy-start(f32[1024]{0:T(1024)} %param.26) | copy-start | bytes 12292
  141.4 84.4 %copy-start.1 = (bf16[256,128]{1,0:T(8,128)(2,1)S(1)}, bf16[256,128]{1,0:T(8,128)(2,1)}, u32[]{:S(2)}) copy-start(bf16[256,128]{1,0:T(8,128)(2,1)} %param.25) | copy-start | bytes 196612
  145.1 177.0 %copy-start.5 = (f32[1024]{0:T(1024)S(1)}, f32[1024]{0:T(1024)}, u32[]{:S(2)}) copy-start(f32[1024]{0:T(1024)} %param.29) | copy-start | bytes 12292
  145.1 177.0 %copy-start.6 = (f32[1024]{0:T(1024)S(1)}, f32[1024]{0:T(1024)}, u32[]{:S(2)}) copy-start(f32[1024]{0:T(1024)} %param.28) | copy-start | bytes 12292
  147.7 139.2 %reduce-scatter.2.cloned.1.call-start = ((), (), s32[]{:S(2)}) async-start(), calls=%async_computation.3 | async-start | bytes 221184 | tf_op jit(solution)/shard_map/reduce_scatter | solution.py:256
  225.7 94.2 %all-reduce.5.cloned.1.call-start = ((), (), s32[]{:S(2)}) async-start(), calls=%async_computation.4 | async-start | bytes 393216 | tf_op jit(solution)/shard_map/psum | solution.py:21
Sparse Core Ops, SparseCore 0:
  10.0 55.8 all-gather.1
  147.8 30.1 all-reduce.2
  225.9 60.9 reduce-scatter.1
  289.2 30.7 all-reduce.4

commit v2 on v1

--- a/solution.py
+++ b/solution.py
@@ -17,13 +17,247 @@
     return center * lax.rsqrt(spread + 1e-05) * gain_row + bias_row
 
 
-def head_total(partial_value):
-    return lax.psum(partial_value, "head")
-
-
 LANES = 128
 NEG = -1e30
 VMEM_LIMIT = 60 * 1024 * 1024
+MESH = pl.DeviceIdType.MESH
+IN_VMEM = pl.BlockSpec(memory_space=pltpu.VMEM)
+
+
+def greet(peers):
+    barrier = pltpu.get_barrier_semaphore()
+    for peer in peers:
+        pl.semaphore_signal(barrier, inc=1, device_id=peer, device_id_type=MESH)
+    pl.semaphore_wait(barrier, len(peers))
+
+
+def others(axis, size):
+    me = lax.axis_index(axis)
+    return [{axis: lax.rem(me + step, size)} for step in range(1, size)]
+
+
+def send(source, target, send_sem, recv_sem, peer):
+    copy = pltpu.make_async_remote_copy(
+        src_ref=source,
+        dst_ref=target,
+        send_sem=send_sem,
+        recv_sem=recv_sem,
+        device_id=peer,
+        device_id_type=MESH,
+    )
+    copy.start()
+    return copy
+
+
+def weights_kernel(size, tokens_ref, *refs):
+    count = 4
+    shards, qkv_ref = refs[:count], refs[count]
+    fulls = (refs[2 * count],) + tuple(refs[count + 1 : 2 * count])
+    send_sems, recv_sems, own_sems = refs[2 * count + 1 :]
+    side = size // 4 if size % 4 == 0 else 1
+    deep = size // side
+    me = lax.axis_index("req")
+    far, near = me // side, lax.rem(me, side)
+    far_peers = [lax.rem(far + step, deep) * side + near for step in range(1, deep)]
+    near_peers = [far * side + lax.rem(near + step, side) for step in range(1, side)]
+    greet([{"req": peer} for peer in far_peers + near_peers])
+
+    def place(which, owner):
+        rows = shards[which].shape[0]
+        if len(fulls[which].shape) == 3:
+            return fulls[which].at[owner]
+        return fulls[which].at[pl.ds(pl.multiple_of(owner * rows, rows), rows), :]
+
+    first = [[], [], [], []]
+    second = [[], [], [], []]
+    own = []
+    for which in range(count):
+        keep = pltpu.make_async_copy(shards[which], place(which, me), own_sems.at[which])
+        keep.start()
+        own.append(keep)
+        for index, peer in enumerate(far_peers + near_peers):
+            first[which].append(
+                send(
+                    shards[which],
+                    place(which, me),
+                    send_sems.at[which, index],
+                    recv_sems.at[which, index],
+                    {"req": peer},
+                )
+            )
+
+    def forward(which):
+        index = deep - 1 + side - 1
+        for step in range(1, deep):
+            first[which][step - 1].wait_recv()
+            owner = lax.rem(far - step + deep, deep) * side + near
+            for peer in near_peers:
+                second[which].append(
+                    send(
+                        place(which, owner),
+                        place(which, owner),
+                        send_sems.at[which, index],
+                        recv_sems.at[which, index],
+                        {"req": peer},
+                    )
+                )
+                index += 1
+
+    for which in range(count):
+        forward(which)
+    for which in range(count):
+        own[which].wait()
+        for copy in first[which][deep - 1 :]:
+            copy.wait_recv()
+        for copy in second[which]:
+            copy.wait_recv()
+        if which == 0:
+            qkv_ref[...] = jnp.dot(
+                tokens_ref[...], fulls[0][...], preferred_element_type=jnp.float32
+            ).astype(qkv_ref.dtype)
+    for which in range(count):
+        for copy in first[which] + second[which]:
+            copy.wait_send()
+
+
+def gather_weights(size, tokens, w_in, w_query, w_out, w_cross):
+    rows = tokens.shape[0]
+    side = size // 4 if size % 4 == 0 else 1
+    deep = size // side
+    copies = (deep - 1) + (side - 1) + (deep - 1) * (side - 1)
+    kind = jnp.bfloat16
+    return pl.pallas_call(
+        functools.partial(weights_kernel, size),
+        out_shape=(
+            jax.ShapeDtypeStruct((rows, w_in.shape[1]), kind),
+            jax.ShapeDtypeStruct((size * w_query.shape[0], w_query.shape[1]), kind),
+            jax.ShapeDtypeStruct((size,) + w_out.shape, kind),
+            jax.ShapeDtypeStruct((size,) + w_cross.shape, kind),
+        ),
+        in_specs=[IN_VMEM] * 5,
+        out_specs=(IN_VMEM,) * 4,
+        scratch_shapes=[
+            pltpu.VMEM((size * w_in.shape[0], w_in.shape[1]), kind),
+            pltpu.SemaphoreType.DMA((4, copies)),
+            pltpu.SemaphoreType.DMA((4, copies)),
+            pltpu.SemaphoreType.DMA((4,)),
+        ],
+        compiler_params=pltpu.CompilerParams(
+            collective_id=0, has_side_effects=True, vmem_limit_bytes=VMEM_LIMIT
+        ),
+        name="gather_weights",
+    )(tokens, w_in, w_query, w_out, w_cross)
+
+
+def spread_and_sum(heads_size, partial, slots_ref, send_sems, recv_sems):
+    me = lax.axis_index("head")
+    slots_ref[me] = partial.astype(slots_ref.dtype)
+    copies = [
+        send(slots_ref.at[me], slots_ref.at[me], send_sems.at[index], recv_sems.at[index], peer)
+        for index, peer in enumerate(others("head", heads_size))
+    ]
+    for copy in copies:
+        copy.wait()
+    summed = slots_ref[0].astype(jnp.float32)
+    for index in range(1, heads_size):
+        summed += slots_ref[index].astype(jnp.float32)
+    return summed
+
+
+def first_kernel(size, heads_size, scale, ctx_ref, tokens_ref, w_out_ref, w_query_ref, gain_ref, bias_ref,
+                 h_ref, queries_ref, slots_ref, head_send, head_recv, req_send, req_recv):
+    greet(others("head", heads_size) + others("req", size))
+    partial = jnp.dot(ctx_ref[...], w_out_ref[...], preferred_element_type=jnp.float32)
+    summed = spread_and_sum(heads_size, partial, slots_ref, head_send, head_recv)
+    h_first = layer_norm(
+        tokens_ref[...].astype(jnp.float32) + summed, gain_ref[...], bias_ref[...]
+    ).astype(jnp.bfloat16)
+    h_ref[...] = h_first
+    query = jnp.dot(h_first, w_query_ref[...], preferred_element_type=jnp.float32)
+    query = query.astype(jnp.bfloat16).astype(jnp.float32) * scale
+    rows = ctx_ref.shape[0]
+    me = lax.axis_index("req")
+    here = pl.ds(pl.multiple_of(me * rows, rows), rows)
+    queries_ref[here, :] = query.astype(jnp.bfloat16)
+    copies = [
+        send(queries_ref.at[here, :], queries_ref.at[here, :], req_send.at[index], req_recv.at[index], peer)
+        for index, peer in enumerate(others("req", size))
+    ]
+    for copy in copies:
+        copy.wait()
+
+
+def last_kernel(size, heads_size, placed_ref, h_ref, w_cross_ref, gain_ref, bias_ref,
+                out_ref, blocks_ref, slots_ref, head_send, head_recv, req_send, req_recv):
+    greet(others("head", heads_size) + others("req", size))
+    rows = h_ref.shape[0]
+    me = lax.axis_index("req")
+    copies = []
+    for index, peer in enumerate(others("req", size)):
+        there = pl.ds(pl.multiple_of(peer["req"] * rows, rows), rows)
+        copies.append(
+            send(placed_ref.at[there, :], blocks_ref.at[me], req_send.at[index], req_recv.at[index], peer)
+        )
+    blocks_ref[me] = placed_ref[pl.ds(pl.multiple_of(me * rows, rows), rows), :]
+    for copy in copies:
+        copy.wait()
+    ctx = blocks_ref[0].astype(jnp.float32)
+    for index in range(1, size):
+        ctx += blocks_ref[index].astype(jnp.float32)
+    partial = jnp.dot(ctx.astype(jnp.bfloat16), w_cross_ref[...], preferred_element_type=jnp.float32)
+    summed = spread_and_sum(heads_size, partial, slots_ref, head_send, head_recv)
+    out_ref[...] = layer_norm(
+        h_ref[...].astype(jnp.float32) + summed, gain_ref[...], bias_ref[...]
+    ).astype(jnp.bfloat16)
+
+
+def exchange_sems(size, heads_size):
+    return [
+        pltpu.SemaphoreType.DMA((heads_size - 1,)),
+        pltpu.SemaphoreType.DMA((heads_size - 1,)),
+        pltpu.SemaphoreType.DMA((size - 1,)),
+        pltpu.SemaphoreType.DMA((size - 1,)),
+    ]
+
+
+def first_half(size, heads_size, scale, ctx, tokens, w_out, w_query, gain, bias):
+    rows, width = tokens.shape
+    cols = ctx.shape[1]
+    return pl.pallas_call(
+        functools.partial(first_kernel, size, heads_size, scale),
+        out_shape=(
+            jax.ShapeDtypeStruct((rows, width), jnp.bfloat16),
+            jax.ShapeDtypeStruct((size * rows, cols), jnp.bfloat16),
+        ),
+        in_specs=[IN_VMEM] * 6,
+        out_specs=(IN_VMEM,) * 2,
+        scratch_shapes=[pltpu.VMEM((heads_size, rows, width), jnp.bfloat16)]
+        + exchange_sems(size, heads_size),
+        compiler_params=pltpu.CompilerParams(
+            collective_id=1, has_side_effects=True, vmem_limit_bytes=VMEM_LIMIT
+        ),
+        name="first_half",
+    )(ctx, tokens, w_out, w_query, gain.reshape(1, -1), bias.reshape(1, -1))
+
+
+def last_half(size, heads_size, placed, h_first, w_cross, gain, bias):
+    rows, width = h_first.shape
+    cols = placed.shape[1]
+    return pl.pallas_call(
+        functools.partial(last_kernel, size, heads_size),
+        out_shape=jax.ShapeDtypeStruct((rows, width), jnp.bfloat16),
+        in_specs=[IN_VMEM] * 5,
+        out_specs=IN_VMEM,
+        scratch_shapes=[
+            pltpu.VMEM((size, rows, cols), jnp.bfloat16),
+            pltpu.VMEM((heads_size, rows, width), jnp.bfloat16),
+        ]
+        + exchange_sems(size, heads_size),
+        compiler_params=pltpu.CompilerParams(
+            collective_id=2, has_side_effects=True, vmem_limit_bytes=VMEM_LIMIT
+        ),
+        name="last_half",
+    )(placed, h_first, w_cross, gain.reshape(1, -1), bias.reshape(1, -1))
 
 
 def pair_copies(source, rows, start, held, sems, slot):
@@ -50,34 +284,43 @@
             copy.start()
     head_row = lax.broadcasted_iota(jnp.int32, (8, cols), 0)
     head_mask = head_row == lax.broadcasted_iota(jnp.int32, (8, cols), 1) // HEAD_DIM
-    column = lax.broadcasted_iota(jnp.int32, (8, span), 1)
+    column = lax.broadcasted_iota(jnp.int32, (8 * batch, span), 1)
     is_key = column % 2 == 0
+
+    def states_of(slot, page):
+        return jnp.concatenate(
+            [held[slot, half, pl.ds(page * span, span), :] for half in range(held.shape[1])], axis=1
+        )
 
     def body(step, carry):
         slot = lax.rem(step, slots)
         for copy in pair_copies(source, rows, step * rows, held, sems, slot):
             copy.wait()
+        stack, limits = [], []
+        for page in range(batch):
+            query = query_ref[pl.ds(step * batch + page, 1), :]
+            spread = jnp.where(head_mask, jnp.broadcast_to(query, (8, cols)), 0.0).astype(jnp.bfloat16)
+            stack.append(
+                lax.dot_general(
+                    spread,
+                    states_of(slot, page),
+                    (((1,), (1,)), ((), ())),
+                    preferred_element_type=jnp.float32,
+                )
+            )
+            limits.append(jnp.full((8, span), 2 * valid_ref[step * batch + page], jnp.int32))
+        counted = is_key & (column < jnp.concatenate(limits, axis=0))
+        scores = jnp.where(counted, jnp.concatenate(stack, axis=0), NEG)
+        top = jnp.max(scores, axis=1, keepdims=True)
+        weights = jnp.where(counted, jnp.exp(scores - top), 0.0)
+        total = jnp.sum(weights, axis=1, keepdims=True)
+        moved = pltpu.roll(weights, 1, 1).astype(jnp.bfloat16)
         accs, tops, totals = [], [], []
         for page in range(batch):
-            valid = valid_ref[step * batch + page]
-            states = jnp.concatenate(
-                [held[slot, half, pl.ds(page * span, span), :] for half in range(held.shape[1])], axis=1
-            )
-            query = query_ref[pl.ds(step * batch + page, 1), :]
-            spread = jnp.where(head_mask, jnp.broadcast_to(query, (8, cols)), 0.0).astype(jnp.bfloat16)
-            scores = lax.dot_general(
-                spread, states, (((1,), (1,)), ((), ())), preferred_element_type=jnp.float32
-            )
-            counted = is_key & (column < 2 * valid)
-            scores = jnp.where(counted, scores, NEG)
-            top = jnp.max(scores, axis=1, keepdims=True)
-            weights = jnp.where(counted, jnp.exp(scores - top), 0.0)
-            total = jnp.sum(weights, axis=1, keepdims=True)
-            moved = pltpu.roll(weights, 1, 1).astype(jnp.bfloat16)
-            summed = jnp.dot(moved, states, preferred_element_type=jnp.float32)
-            accs.append(jnp.sum(jnp.where(head_mask, summed, 0.0), axis=0, keepdims=True))
-            tops.append(jnp.sum(jnp.where(head_mask, top, 0.0), axis=0, keepdims=True))
-            totals.append(jnp.sum(jnp.where(head_mask, total, 0.0), axis=0, keepdims=True))
+            mine = slice(8 * page, 8 * page + 8)
+            summed = jnp.dot(moved[mine], states_of(slot, page), preferred_element_type=jnp.float32)
+            for parts, value in ((accs, summed), (tops, top[mine]), (totals, total[mine])):
+                parts.append(jnp.sum(jnp.where(head_mask, value, 0.0), axis=0, keepdims=True))
         here = pl.ds(pl.multiple_of(step * batch, batch), batch)
         acc_ref[here, :] = jnp.concatenate(accs, axis=0)
         top_ref[here, :] = jnp.concatenate(tops, axis=0)
@@ -95,8 +338,8 @@
 
 def page_parts(page_valid, page_query, kv_pool):
     pages, page_rows, _, cols = kv_pool.shape
-    batch = 8
-    slots = min(8, pages // batch)
+    batch = 16
+    slots = min(4, pages // batch)
     part = jax.ShapeDtypeStruct((pages, cols), jnp.float32)
     return pl.pallas_call(
         functools.partial(page_kernel, batch=batch),
@@ -248,15 +491,9 @@
     return picker.astype(jnp.bfloat16).reshape(groups_here * GMAX, -1)
 
 
-def group_attention(cross_query, group_of, enc_kv, scale):
-    scaled = (cross_query * scale).astype(jnp.bfloat16)
-    every_query = lax.all_gather(scaled, "req", axis=0, tiled=True)
-    picker = group_picker(group_of, enc_kv.shape[0])
-    placed = group_parts(picker, every_query, enc_kv)
-    return lax.psum_scatter(placed, "req", scatter_dimension=0, tiled=True)
-
-
 def on_device(
+    size,
+    heads_size,
     tokens,
     cache_len,
     page_table,
@@ -277,36 +514,33 @@
     width = tokens.shape[1]
     head_cols = kv_pool.shape[3]
     scale = HEAD_DIM ** (-0.5)
-    full_in, full_out, full_query, full_cross = (
-        lax.all_gather(w_self_in, "req", axis=0, tiled=True),
-        lax.all_gather(w_self_out, "req", axis=1, tiled=True),
-        lax.all_gather(w_cross_q, "req", axis=0, tiled=True),
-        lax.all_gather(w_cross_out, "req", axis=1, tiled=True),
-    )
-    projected = jnp.dot(
-        tokens, full_in.reshape(width, 3 * head_cols), preferred_element_type=jnp.float32
-    )
-    qkv = projected.astype(jnp.bfloat16).reshape(rows_here, 3, head_cols)
+    projected, full_query, out_blocks, cross_blocks = gather_weights(
+        size, tokens, w_self_in.reshape(w_self_in.shape[0], 3 * head_cols), w_cross_q, w_self_out, w_cross_out
+    )
+    full_out = out_blocks.transpose(1, 0, 2).reshape(head_cols, width)
+    full_cross = cross_blocks.transpose(1, 0, 2).reshape(head_cols, width)
+    qkv = projected.reshape(rows_here, 3, head_cols)
     self_ctx = paged_attention(
-        qkv[:, 0], qkv[:, 1], qkv[:, 2], cache_len, page_table, page_live, kv_pool, scale
-    )
-    self_proj = head_total(jnp.dot(self_ctx, full_out, preferred_element_type=jnp.float32))
-    h_first = layer_norm(tokens.astype(jnp.float32) + self_proj, self_gain, self_bias).astype(
-        jnp.bfloat16
-    )
-    cross_query = jnp.dot(h_first, full_query, preferred_element_type=jnp.float32)
-    cross_query = cross_query.astype(jnp.bfloat16)
-    cross_ctx = group_attention(cross_query, group_of, enc_kv, scale)
-    cross_proj = head_total(jnp.dot(cross_ctx, full_cross, preferred_element_type=jnp.float32))
-    hidden_out = layer_norm(
-        h_first.astype(jnp.float32) + cross_proj, cross_gain, cross_bias
-    ).astype(jnp.bfloat16)
+        projected[:, :head_cols],
+        projected[:, head_cols : 2 * head_cols],
+        projected[:, 2 * head_cols :],
+        cache_len,
+        page_table,
+        page_live,
+        kv_pool,
+        scale,
+    )
+    h_first, every_query = first_half(
+        size, heads_size, scale, self_ctx, tokens, full_out, full_query, self_gain, self_bias
+    )
+    placed = group_parts(group_picker(group_of, enc_kv.shape[0]), every_query, enc_kv)
+    hidden_out = last_half(size, heads_size, placed, h_first, full_cross, cross_gain, cross_bias)
     return (hidden_out, qkv[:, 1:3])
 
 
 def solution(mesh):
     return jax.shard_map(
-        on_device,
+        functools.partial(on_device, mesh.shape["req"], mesh.shape["head"]),
         mesh=mesh,
         in_specs=(
             P("req", None),

time: 331 us -> 130 us (0.39)
  blocking collectives: 124 us -> 0 us
  waiting for transfers between devices: 93.5 us -> 0 us
  Pallas kernels: 71 us -> 108 us
  between operations: 14 us -> 0.83 us
  other arithmetic: 16.2 us -> 9.32 us
  matrix products: 7.27 us -> 3.26 us
  local copies, waits for them, and re-layouts: 3.98 us -> 7.44 us
    all_gather x4 -> x0, blocking collectives: 124 us -> none  [the longest x1 32.8 us: on_device(): lax.all_gather(w_cross_q, 'req', axis=0, tiled=True)]
    pallas_call x0 -> x3, Pallas kernels: none -> 83.8 us  [the longest x1 49.4 us: gather_weights(): pl.pallas_call(functools.partial(weights_kernel, size), out_shape=(jax.Sh...]
    psum x2 -> x0, waiting for transfers between devices: 60.1 us -> none  [head_total(): return lax.psum(partial_value, 'head')]
    pallas_call x1, Pallas kernels: 59.5 us -> 12.7 us  [page_parts(): pl.pallas_call(functools.partial(page_kernel, batch=batch), out_shape=(pa...]
    reduce_scatter x1 -> x0, waiting for transfers between devices: 33.3 us -> none  [group_attention(): return lax.psum_scatter(placed, 'req', scatter_dimension=0, tiled=True)]
    dot_general x4 -> x0, matrix products: 4.76 us -> none  [the longest x1 2.05 us: on_device(): jnp.dot(tokens, full_in.reshape(width, 3 * head_cols), preferred_element_...]
    reduce_sum x4 -> x0, other arithmetic: 4.37 us -> none  [the longest x2 2.25 us: layer_norm(): spread = jnp.mean(center * center, axis=-1, keepdims=True)]
  transfers between devices with their start and end apart: 4 -> 0, of which waited for: 3 -> 0; matrix products, arithmetic and copies ran while one was open for 2% -> 0% of each run, Pallas kernels for 0% -> 0%
where the time goes in v2:
time: 130 us; the launch traced here: 129 us
  Pallas kernels  108 us (83%)
  other arithmetic  9.32 us (7%)
  local copies, waits for them, and re-layouts  7.44 us (6%)
  matrix products  3.26 us (3%)
    pallas_call x1, Pallas kernels, gather_weights(): pl.pallas_call(functools.partial(weights_kernel, size), out_shape=(jax.Sh...  49.4 us
    pallas_call x1, Pallas kernels, first_half(): pl.pallas_call(functools.partial(first_kernel, size, heads_size, scale),...  19.6 us
    pallas_call x1, Pallas kernels, last_half(): pl.pallas_call(functools.partial(last_kernel, size, heads_size), out_shap...  14.8 us
    pallas_call x1, Pallas kernels, page_parts(): pl.pallas_call(functools.partial(page_kernel, batch=batch), out_shape=(pa...  12.7 us
    pallas_call x1, Pallas kernels, group_parts(): pl.pallas_call(group_kernel, out_shape=jax.ShapeDtypeStruct(queries.shape...  11.5 us
    reduce_max x1, other arithmetic, paged_attention(): jnp.max(jnp.where(counted[:, :, None], page_top[None, :, :], NEG), axis=1)  3.66 us
    unnamed x14, local copies, waits for them, and re-layouts  3.42 us

profile of v2, /device:TPU:0, one launch (start us, length us, event | category | flops | bytes accessed | tf_op | source)
XLA Modules:
  0.0 128.8 jit_solution(12808312477231177654)
XLA Ops:
  0.6 1.1 copy.30
  1.7 0.8 copy.31.refs_0_
  2.5 49.4 %gather_weights.1 = (bf16[48,768]{1,0:T(8,128)(2,1)}, bf16[1024,256]{1,0:T(8,128)(2,1)}, bf16[8,256,128]{2,1,0:T(8,128)(2,1)}, bf16[8,256,128]{2,1,0:T(8,128)(2,1)}) custom-call(bf16[48,1024]{1,0:T(8,128)(2,1)} %tokens_ref.3, bf16[128,768]{1,0:T(8,128)(2,1)} %copy.31.refs_0_, bf16[128,256]{1,0:T(8,128)(2,1)} %refs_1_.1, bf16[256,128]{1,0:T(8,128)(2,1)} %refs_2_.1, ...), custom_call_target="tpu_custom_call" | custom-call | tf_op jit(solution)/shard_map/gather_weights/pallas_call | solution.py:129
  51.9 0.8 copy.28
  52.7 0.7 and_select_fusion
  53.3 0.1 iota_compare_fusion.1
  53.4 0.2 fusion.3
  53.6 1.6 %fusion.13.query_ref = f32[160,256]{1,0:T(8,128)} fusion(pred[48,160]{1,0:T(8,128)(4,1)S(1)} %fusion.3, bf16[48,768]{1,0:T(8,128)(2,1)} %get-tuple-element.11), kind=kOutput, calls=%fused_computation.24 | convolution fusion | flops 3944448 | bytes 196096 | tf_op jit(solution)/shard_map/dot_general | solution.py:387
  55.3 0.8 clamp_select_fusion
  56.0 0.1 copy.29
  56.1 0.8 select_reduce_fusion.1.valid_ref
  56.9 0.0 copy-start.4
  56.9 0.0 copy-start.2
  56.9 0.0 copy-start.1
  56.9 0.0 copy-start.3
  56.9 12.7 %page_parts.1 = (f32[160,256]{1,0:T(8,128)}, f32[160,256]{1,0:T(8,128)}, f32[160,256]{1,0:T(8,128)}) custom-call(s32[160]{0:T(256)} %select_reduce_fusion.1.valid_ref, f32[160,256]{1,0:T(8,128)} %fusion.13.query_ref, bf16[160,128,2,256]{3,2,1,0:T(2,128)(2,1)} %kv_ref.2), custom_call_target="tpu_custom_call" | custom-call | flops 335544320 | bytes 20971520 | tf_op jit(solution)/shard_map/page_parts/pallas_call | solution.py:344
  69.7 0.0 copy-start
  69.7 0.0 copy-done.4
  69.7 3.7 %select_reduce_fusion = f32[48,256]{1,0:T(8,128)S(1)} fusion(f32[160,256]{1,0:T(8,128)} %get-tuple-element.13, pred[48,160]{1,0:T(8,128)(4,1)S(1)} %broadcast_and_fusion), kind=kLoop, calls=%fused_computation | loop fusion | flops 3919872 | bytes 220672 | tf_op jit(solution)/shard_map/reduce_max | solution.py:393
  73.4 0.0 copy-done.2
  73.4 0.1 reshape.147
  73.5 0.1 reduce_sum.19
  73.7 0.1 broadcast_in_dim.72
  73.8 0.1 reshape.148
  73.9 1.4 %fusion.20 = (f32[160,256]{1,0:T(8,128)S(1)}, f32[160,256]{1,0:T(8,128)S(1)}) fusion(f32[160,256]{1,0:T(8,128)} %get-tuple-element.12, f32[160,256]{1,0:T(8,128)} %get-tuple-element.14, f32[160,256]{1,0:T(8,128)} %get-tuple-element.13, pred[48,160]{1,0:T(8,128)(4,1)S(1)} %fusion.3, f32[48,256]{1,0:T(8,128)S(1)} %select_reduce_fusion, ...), kind=kOutput, calls=%fused_computation.47 | convolution fusion | flops 23769088 | bytes 925344 | tf_op jit(solution)/shard_map/dot_general | solution.py:395
  75.3 0.3 fusion.4
  75.6 0.6 fusion.11.ctx_ref
  76.2 0.0 copy-done.1
  76.2 0.9 copy_bitcast_fusion.1.w_out_ref
  77.1 19.6 %first_half.1 = (bf16[48,1024]{1,0:T(8,128)(2,1)}, bf16[384,256]{1,0:T(8,128)(2,1)}) custom-call(bf16[48,256]{1,0:T(8,128)(2,1)} %fusion.11.ctx_ref, bf16[48,1024]{1,0:T(8,128)(2,1)} %tokens_ref.3, bf16[256,1024]{1,0:T(8,128)(2,1)} %copy_bitcast_fusion.1.w_out_ref, bf16[1024,256]{1,0:T(8,128)(2,1)} %get-tuple-element.16.w_query_ref, f32[1,1024]{1,0:T(1,128)} %bitcast.39, ...), custom_call_target="tpu_custom_call" | custom-call | tf_op jit(solution)/shard_map/first_half/pallas_call | solution.py:226
  96.7 0.0 copy-done.3
  96.7 0.1 compare_convert_fusion
  96.8 1.2 reduce-window.6
  98.0 0.2 slice_reduce_fusion
  98.2 0.2 reduce-window.9
  98.4 0.1 add_bitcast_fusion
  98.5 0.1 broadcast_compare_fusion
  98.6 0.1 eq.75
  98.6 0.7 fusion.9.picker_ref
  99.4 11.5 %group_parts.1.placed_ref = bf16[384,256]{1,0:T(8,128)(2,1)} custom-call(bf16[64,384]{1,0:T(8,128)(2,1)} %fusion.9.picker_ref, bf16[384,256]{1,0:T(8,128)(2,1)} %get-tuple-element.17.query_ref, bf16[4,2048,2,256]{3,2,1,0:T(2,128)(2,1)} %kv_ref.3), custom_call_target="tpu_custom_call" | custom-call | tf_op jit(solution)/shard_map/group_parts/pallas_call | solution.py:465
  110.9 0.0 copy-done
  110.9 0.9 copy_bitcast_fusion.w_cross_ref
  111.8 14.8 %last_half.1 = bf16[48,1024]{1,0:T(8,128)(2,1)} custom-call(bf16[384,256]{1,0:T(8,128)(2,1)} %group_parts.1.placed_ref, bf16[48,1024]{1,0:T(8,128)(2,1)} %get-tuple-element.18.h_ref, bf16[256,1024]{1,0:T(8,128)(2,1)} %copy_bitcast_fusion.w_cross_ref, f32[1,1024]{1,0:T(1,128)} %bitcast.41, f32[1,1024]{1,0:T(1,128)} %bitcast.42), custom_call_target="tpu_custom_call" | custom-call | tf_op jit(solution)/shard_map/last_half/pallas_call | solution.py:246
  126.6 0.7 slice.35
  127.3 1.5 %copy.42 = bf16[48,1024]{1,0:T(8,128)(2,1)} copy(bf16[48,1024]{1,0:T(8,128)(2,1)} %last_half.1) | data formatting | bytes 196608
  (10 shorter events, 0.1 us)
Async XLA Ops:
  56.9 12.7 %copy-start.4 = (s32[160]{0:T(256)S(1)}, s32[160]{0:T(256)}, u32[]{:S(2)}) copy-start(s32[160]{0:T(256)} %select_reduce_fusion.1.valid_ref) | copy-start | bytes 1924
  56.9 16.4 %copy-start.2 = (bf16[48,768]{1,0:T(8,128)(2,1)S(1)}, bf16[48,768]{1,0:T(8,128)(2,1)}, u32[]{:S(2)}) copy-start(bf16[48,768]{1,0:T(8,128)(2,1)} %get-tuple-element.11) | copy-start | bytes 221188
  56.9 19.3 %copy-start.1 = (bf16[8,256,128]{2,1,0:T(8,128)(2,1)S(1)}, bf16[8,256,128]{2,1,0:T(8,128)(2,1)}, u32[]{:S(2)}) copy-start(bf16[8,256,128]{2,1,0:T(8,128)(2,1)} %get-tuple-element.15) | copy-start | bytes 1572868
  56.9 39.8 %copy-start.3 = (s32[384]{0:T(512)S(1)}, s32[384]{0:T(512)}, u32[]{:S(2)}) copy-start(s32[384]{0:T(512)} %param.19) | copy-start | bytes 4612
  69.7 41.2 %copy-start = (bf16[8,256,128]{2,1,0:T(8,128)(2,1)S(1)}, bf16[8,256,128]{2,1,0:T(8,128)(2,1)}, u32[]{:S(2)}) copy-start(bf16[8,256,128]{2,1,0:T(8,128)(2,1)} %get-tuple-element.19) | copy-start | bytes 1572868

commit v3 on v2

--- a/solution.py
+++ b/solution.py
@@ -49,104 +49,101 @@
     return copy
 
 
-def weights_kernel(size, tokens_ref, *refs):
-    count = 4
-    shards, qkv_ref = refs[:count], refs[count]
-    fulls = (refs[2 * count],) + tuple(refs[count + 1 : 2 * count])
-    send_sems, recv_sems, own_sems = refs[2 * count + 1 :]
-    side = size // 4 if size % 4 == 0 else 1
-    deep = size // side
-    me = lax.axis_index("req")
-    far, near = me // side, lax.rem(me, side)
-    far_peers = [lax.rem(far + step, deep) * side + near for step in range(1, deep)]
-    near_peers = [far * side + lax.rem(near + step, side) for step in range(1, side)]
-    greet([{"req": peer} for peer in far_peers + near_peers])
-
-    def place(which, owner):
-        rows = shards[which].shape[0]
-        if len(fulls[which].shape) == 3:
-            return fulls[which].at[owner]
-        return fulls[which].at[pl.ds(pl.multiple_of(owner * rows, rows), rows), :]
-
-    first = [[], [], [], []]
-    second = [[], [], [], []]
-    own = []
-    for which in range(count):
-        keep = pltpu.make_async_copy(shards[which], place(which, me), own_sems.at[which])
-        keep.start()
-        own.append(keep)
-        for index, peer in enumerate(far_peers + near_peers):
-            first[which].append(
-                send(
-                    shards[which],
-                    place(which, me),
-                    send_sems.at[which, index],
-                    recv_sems.at[which, index],
-                    {"req": peer},
-                )
+class Relay:
+    def __init__(self, size, shards, fulls, send_sems, recv_sems, own_sems):
+        self.side = size // 4 if size % 4 == 0 else 1
+        self.deep = size // self.side
+        self.shards, self.fulls = shards, fulls
+        self.sems = (send_sems, recv_sems, own_sems)
+        side, deep, me = self.side, self.deep, lax.axis_index("req")
+        self.me, self.far, self.near = me, me // side, lax.rem(me, side)
+        self.far_peers = [lax.rem(self.far + step, deep) * side + self.near for step in range(1, deep)]
+        self.near_peers = [self.far * side + lax.rem(self.near + step, side) for step in range(1, side)]
+        self.peers = self.far_peers + self.near_peers
+
+    def place(self, which, owner):
+        full, rows = self.fulls[which], self.shards[which].shape[0]
+        if len(full.shape) == 3:
+            return full.at[owner]
+        return full.at[pl.ds(pl.multiple_of(owner * rows, rows), rows), :]
+
+    def push(self, which, index, source, owner, peer):
+        send_sems, recv_sems, _ = self.sems
+        return send(
+            source,
+            self.place(which, owner),
+            send_sems.at[which, index],
+            recv_sems.at[which, index],
+            {"req": peer},
+        )
+
+    def start(self):
+        greet([{"req": peer} for peer in self.peers])
+        self.first, self.second, self.own = [], [], []
+        for which, shard in enumerate(self.shards):
+            keep = pltpu.make_async_copy(shard, self.place(which, self.me), self.sems[2].at[which])
+            keep.start()
+            self.own.append(keep)
+            self.first.append(
+                [self.push(which, index, shard, self.me, peer) for index, peer in enumerate(self.peers)]
             )
 
-    def forward(which):
-        index = deep - 1 + side - 1
-        for step in range(1, deep):
-            first[which][step - 1].wait_recv()
-            owner = lax.rem(far - step + deep, deep) * side + near
-            for peer in near_peers:
-                second[which].append(
-                    send(
-                        place(which, owner),
-                        place(which, owner),
-                        send_sems.at[which, index],
-                        recv_sems.at[which, index],
-                        {"req": peer},
-                    )
-                )
-                index += 1
-
-    for which in range(count):
-        forward(which)
-    for which in range(count):
-        own[which].wait()
-        for copy in first[which][deep - 1 :]:
-            copy.wait_recv()
-        for copy in second[which]:
-            copy.wait_recv()
-        if which == 0:
-            qkv_ref[...] = jnp.dot(
-                tokens_ref[...], fulls[0][...], preferred_element_type=jnp.float32
-            ).astype(qkv_ref.dtype)
-    for which in range(count):
-        for copy in first[which] + second[which]:
-            copy.wait_send()
-
-
-def gather_weights(size, tokens, w_in, w_query, w_out, w_cross):
-    rows = tokens.shape[0]
+    def forward(self):
+        for which in range(len(self.shards)):
+            index = len(self.peers)
+            passed = []
+            for step in range(1, self.deep):
+                self.first[which][step - 1].wait_recv()
+                owner = lax.rem(self.far - step + self.deep, self.deep) * self.side + self.near
+                for peer in self.near_peers:
+                    passed.append(self.push(which, index, self.place(which, owner), owner, peer))
+                    index += 1
+            self.second.append(passed)
+
+    def finish(self):
+        for which in range(len(self.shards)):
+            self.own[which].wait()
+            for copy in self.first[which][self.deep - 1 :] + self.second[which]:
+                copy.wait_recv()
+        for which in range(len(self.shards)):
+            for copy in self.first[which] + self.second[which]:
+                copy.wait_send()
+
+
+def relay_sems(size, count):
     side = size // 4 if size % 4 == 0 else 1
     deep = size // side
     copies = (deep - 1) + (side - 1) + (deep - 1) * (side - 1)
-    kind = jnp.bfloat16
+    return [
+        pltpu.SemaphoreType.DMA((count, copies)),
+        pltpu.SemaphoreType.DMA((count, copies)),
+        pltpu.SemaphoreType.DMA((count,)),
+    ]
+
+
+def project_kernel(size, tokens_ref, w_in_ref, qkv_ref, full_ref, *sems):
+    relay = Relay(size, [w_in_ref], [full_ref], *sems)
+    relay.start()
+    relay.forward()
+    relay.finish()
+    qkv_ref[...] = jnp.dot(
+        tokens_ref[...], full_ref[...], preferred_element_type=jnp.float32
+    ).astype(qkv_ref.dtype)
+
+
+def project(size, tokens, w_in):
     return pl.pallas_call(
-        functools.partial(weights_kernel, size),
-        out_shape=(
-            jax.ShapeDtypeStruct((rows, w_in.shape[1]), kind),
-            jax.ShapeDtypeStruct((size * w_query.shape[0], w_query.shape[1]), kind),
-            jax.ShapeDtypeStruct((size,) + w_out.shape, kind),
-            jax.ShapeDtypeStruct((size,) + w_cross.shape, kind),
-        ),
-        in_specs=[IN_VMEM] * 5,
-        out_specs=(IN_VMEM,) * 4,
-        scratch_shapes=[
-            pltpu.VMEM((size * w_in.shape[0], w_in.shape[1]), kind),
-            pltpu.SemaphoreType.DMA((4, copies)),
-            pltpu.SemaphoreType.DMA((4, copies)),
-            pltpu.SemaphoreType.DMA((4,)),
-        ],
+        functools.partial(project_kernel, size),
+        out_shape=jax.ShapeDtypeStruct((tokens.shape[0], w_in.shape[1]), jnp.bfloat16),
+        in_specs=[IN_VMEM] * 2,
+        out_specs=IN_VMEM,
+        scratch_shapes=[pltpu.VMEM((size * w_in.shape[0], w_in.shape[1]), jnp.bfloat16)]
+        + relay_sems(size, 1),
         compiler_params=pltpu.CompilerParams(
             collective_id=0, has_side_effects=True, vmem_limit_bytes=VMEM_LIMIT
         ),
-        name="gather_weights",
-    )(tokens, w_in, w_query, w_out, w_cross)
+        name="project",
+    )(tokens, w_in)
 
 
 def spread_and_sum(heads_size, partial, slots_ref, send_sems, recv_sems):
@@ -271,7 +268,8 @@
     ]
 
 
-def page_kernel(valid_ref, query_ref, kv_ref, acc_ref, top_ref, total_ref, held, sems, *, batch):
+def page_kernel(valid_ref, query_ref, kv_ref, w_out_ref, w_query_ref, acc_ref, top_ref, total_ref,
+                out_blocks_ref, full_query_ref, held, sems, *relay_refs, batch, size):
     pages, page_rows, _, cols = kv_ref.shape
     heads = cols // HEAD_DIM
     span = 2 * page_rows
@@ -282,6 +280,8 @@
     for step in range(min(slots, steps)):
         for copy in pair_copies(source, rows, step * rows, held, sems, step):
             copy.start()
+    relay = Relay(size, [w_out_ref, w_query_ref], [out_blocks_ref, full_query_ref], *relay_refs)
+    relay.start()
     head_row = lax.broadcasted_iota(jnp.int32, (8, cols), 0)
     head_mask = head_row == lax.broadcasted_iota(jnp.int32, (8, cols), 1) // HEAD_DIM
     column = lax.broadcasted_iota(jnp.int32, (8 * batch, span), 1)
@@ -333,38 +333,54 @@
 
         return carry
 
-    lax.fori_loop(0, steps, body, 0)
-
-
-def page_parts(page_valid, page_query, kv_pool):
+    lax.fori_loop(0, steps // 2, body, 0)
+    relay.forward()
+    lax.fori_loop(steps // 2, steps, body, 0)
+    relay.finish()
+
+
+def page_parts(size, page_valid, page_query, kv_pool, w_out, w_query):
     pages, page_rows, _, cols = kv_pool.shape
     batch = 16
     slots = min(4, pages // batch)
     part = jax.ShapeDtypeStruct((pages, cols), jnp.float32)
     return pl.pallas_call(
-        functools.partial(page_kernel, batch=batch),
-        out_shape=(part, part, part),
+        functools.partial(page_kernel, batch=batch, size=size),
+        out_shape=(
+            part,
+            part,
+            part,
+            jax.ShapeDtypeStruct((size,) + w_out.shape, jnp.bfloat16),
+            jax.ShapeDtypeStruct((size * w_query.shape[0], w_query.shape[1]), jnp.bfloat16),
+        ),
         in_specs=[
             pl.BlockSpec(memory_space=pltpu.SMEM),
             pl.BlockSpec(memory_space=pltpu.VMEM),
             pl.BlockSpec(memory_space=pl.ANY),
+            IN_VMEM,
+            IN_VMEM,
         ],
-        out_specs=(pl.BlockSpec(memory_space=pltpu.VMEM),) * 3,
+        out_specs=(IN_VMEM,) * 5,
         scratch_shapes=[
             pltpu.VMEM((slots, cols // LANES, batch * 2 * page_rows, LANES), jnp.bfloat16),
             pltpu.SemaphoreType.DMA((slots, cols // LANES)),
-        ],
-        compiler_params=pltpu.CompilerParams(vmem_limit_bytes=VMEM_LIMIT),
+        ]
+        + relay_sems(size, 2),
+        compiler_params=pltpu.CompilerParams(
+            collective_id=3, has_side_effects=True, vmem_limit_bytes=VMEM_LIMIT
+        ),
         cost_estimate=pl.CostEstimate(
             flops=pages * 8 * 2 * page_rows * cols * 4,
             bytes_accessed=pages * page_rows * 4 * cols,
             transcendentals=pages * 16 * page_rows,
         ),
         name="page_parts",
-    )(page_valid, page_query, kv_pool)
-
-
-def paged_attention(query, new_key, new_value, cache_len, page_table, page_live, kv_pool, scale):
+    )(page_valid, page_query, kv_pool, w_out, w_query)
+
+
+def paged_attention(
+    size, query, new_key, new_value, cache_len, page_table, page_live, kv_pool, w_out, w_query, scale
+):
     pages_here, page_rows, _, head_cols = kv_pool.shape
     heads_here = head_cols // HEAD_DIM
     rows_here = query.shape[0]
@@ -385,7 +401,9 @@
     owner_weights = owners.astype(jnp.float32)
     scaled = (query * scale).astype(jnp.bfloat16)
     page_query = jnp.dot(owners.T.astype(jnp.bfloat16), scaled, preferred_element_type=jnp.float32)
-    page_sum, page_top, page_total = page_parts(page_valid, page_query, kv_pool)
+    page_sum, page_top, page_total, out_blocks, full_query = page_parts(
+        size, page_valid, page_query, kv_pool, w_out, w_query
+    )
     products = query.astype(jnp.float32) * new_key.astype(jnp.float32)
     new_score = jnp.sum(products.reshape(rows_here, heads_here, HEAD_DIM), axis=-1) * scale
     new_score = jnp.repeat(new_score, HEAD_DIM, axis=1)
@@ -402,10 +420,12 @@
     )
     rounded_new = lax.optimization_barrier(new_weight.astype(jnp.bfloat16)).astype(jnp.float32)
     summed = both[:, :head_cols] + rounded_new * new_value.astype(jnp.float32)
-    return (summed / (both[:, head_cols:] + new_weight)).astype(jnp.bfloat16)
-
-
-def group_kernel(picker_ref, query_ref, kv_ref, out_ref, held, scores_ref, sems):
+    context = (summed / (both[:, head_cols:] + new_weight)).astype(jnp.bfloat16)
+    return context, out_blocks, full_query
+
+
+def group_kernel(size, picker_ref, query_ref, kv_ref, w_cross_ref, out_ref, cross_blocks_ref,
+                 held, scores_ref, sems, *relay_refs):
     groups, positions, _, cols = kv_ref.shape
     heads = cols // HEAD_DIM
     span = 2 * positions
@@ -413,11 +433,15 @@
     for group in range(groups):
         for copy in pair_copies(source, span, group * span, held, sems, group):
             copy.start()
+    relay = Relay(size, [w_cross_ref], [cross_blocks_ref], *relay_refs)
+    relay.start()
     lane_head = lax.broadcasted_iota(jnp.int32, (GMAX, cols), 1) // HEAD_DIM
     block = min(512, span)
     is_key = lax.broadcasted_iota(jnp.int32, (heads * GMAX, block), 1) % 2 == 0
     placed = jnp.zeros(out_ref.shape, jnp.float32)
     for group in range(groups):
+        if group == groups // 2:
+            relay.forward()
         picker = picker_ref[pl.ds(group * GMAX, GMAX), :]
         query = jnp.dot(picker, query_ref[...], preferred_element_type=jnp.float32)
         spread = jnp.concatenate(
@@ -457,28 +481,36 @@
             preferred_element_type=jnp.float32,
         )
     out_ref[...] = placed.astype(jnp.bfloat16)
-
-
-def group_parts(picker, queries, enc_kv):
+    relay.finish()
+
+
+def group_parts(size, picker, queries, enc_kv, w_cross):
     groups, positions, _, cols = enc_kv.shape
     heads = cols // HEAD_DIM
     return pl.pallas_call(
-        group_kernel,
-        out_shape=jax.ShapeDtypeStruct(queries.shape, jnp.bfloat16),
+        functools.partial(group_kernel, size),
+        out_shape=(
+            jax.ShapeDtypeStruct(queries.shape, jnp.bfloat16),
+            jax.ShapeDtypeStruct((size,) + w_cross.shape, jnp.bfloat16),
+        ),
         in_specs=[
             pl.BlockSpec(memory_space=pltpu.VMEM),
             pl.BlockSpec(memory_space=pltpu.VMEM),
             pl.BlockSpec(memory_space=pl.ANY),
+            IN_VMEM,
         ],
-        out_specs=pl.BlockSpec(memory_space=pltpu.VMEM),
+        out_specs=(IN_VMEM,) * 2,
         scratch_shapes=[
             pltpu.VMEM((groups, cols // LANES, 2 * positions, LANES), jnp.bfloat16),
             pltpu.VMEM((heads * GMAX, 2 * positions), jnp.float32),
             pltpu.SemaphoreType.DMA((groups, cols // LANES)),
-        ],
-        compiler_params=pltpu.CompilerParams(vmem_limit_bytes=VMEM_LIMIT),
+        ]
+        + relay_sems(size, 1),
+        compiler_params=pltpu.CompilerParams(
+            collective_id=4, has_side_effects=True, vmem_limit_bytes=VMEM_LIMIT
+        ),
         name="group_parts",
-    )(picker, queries, enc_kv)
+    )(picker, queries, enc_kv, w_cross)
 
 
 def group_picker(group_of, groups_here):
@@ -514,13 +546,10 @@
     width = tokens.shape[1]
     head_cols = kv_pool.shape[3]
     scale = HEAD_DIM ** (-0.5)
-    projected, full_query, out_blocks, cross_blocks = gather_weights(
-        size, tokens, w_self_in.reshape(w_self_in.shape[0], 3 * head_cols), w_cross_q, w_self_out, w_cross_out
-    )
-    full_out = out_blocks.transpose(1, 0, 2).reshape(head_cols, width)
-    full_cross = cross_blocks.transpose(1, 0, 2).reshape(head_cols, width)
+    projected = project(size, tokens, w_self_in.reshape(w_self_in.shape[0], 3 * head_cols))
     qkv = projected.reshape(rows_here, 3, head_cols)
-    self_ctx = paged_attention(
+    self_ctx, out_blocks, full_query = paged_attention(
+        size,
         projected[:, :head_cols],
         projected[:, head_cols : 2 * head_cols],
         projected[:, 2 * head_cols :],
@@ -528,12 +557,18 @@
         page_table,
         page_live,
         kv_pool,
+        w_self_out,
+        w_cross_q,
         scale,
     )
+    full_out = out_blocks.transpose(1, 0, 2).reshape(head_cols, width)
     h_first, every_query = first_half(
         size, heads_size, scale, self_ctx, tokens, full_out, full_query, self_gain, self_bias
     )
-    placed = group_parts(group_picker(group_of, enc_kv.shape[0]), every_query, enc_kv)
+    placed, cross_blocks = group_parts(
+        size, group_picker(group_of, enc_kv.shape[0]), every_query, enc_kv, w_cross_out
+    )
+    full_cross = cross_blocks.transpose(1, 0, 2).reshape(head_cols, width)
     hidden_out = last_half(size, heads_size, placed, h_first, full_cross, cross_gain, cross_bias)
     return (hidden_out, qkv[:, 1:3])
 

time: 130 us -> 124 us (0.954)
  Pallas kernels: 108 us -> 100 us
  local copies, waits for them, and re-layouts: 7.44 us -> 9.51 us
    pallas_call x1, Pallas kernels: 19.6 us -> 15.7 us  [first_half(): pl.pallas_call(functools.partial(first_kernel, size, heads_size, scale),...]
    pallas_call x3, Pallas kernels: 73.6 us -> 70.6 us  [the longest x1 31.8 us: project(): pl.pallas_call(functools.partial(project_kernel, size), out_shape=jax.Sha...]
    unnamed x14 -> x10, local copies, waits for them, and re-layouts: 3.42 us -> 3.41 us
where the time goes in v3:
time: 124 us; the launch traced here: 123 us
  Pallas kernels  100 us (81%)
  local copies, waits for them, and re-layouts  9.51 us (8%)
  other arithmetic  9.29 us (7%)
  matrix products  3.26 us (3%)
    pallas_call x1, Pallas kernels, project(): pl.pallas_call(functools.partial(project_kernel, size), out_shape=jax.Sha...  31.8 us
    pallas_call x1, Pallas kernels, page_parts(): pl.pallas_call(functools.partial(page_kernel, batch=batch, size=size), ou...  22.8 us
    pallas_call x1, Pallas kernels, group_parts(): pl.pallas_call(functools.partial(group_kernel, size), out_shape=(jax.Shap...  16 us
    pallas_call x1, Pallas kernels, first_half(): pl.pallas_call(functools.partial(first_kernel, size, heads_size, scale),...  15.7 us
    pallas_call x1, Pallas kernels, last_half(): pl.pallas_call(functools.partial(last_kernel, size, heads_size), out_shap...  14 us
    reduce_max x1, other arithmetic, paged_attention(): jnp.max(jnp.where(counted[:, :, None], page_top[None, :, :], NEG), axis=1)  3.62 us
    unnamed x10, local copies, waits for them, and re-layouts  3.41 us

profile of v3, /device:TPU:0, one launch (start us, length us, event | category | flops | bytes accessed | tf_op | source)
XLA Modules:
  0.0 123.1 jit_solution(1034160026187946755)
XLA Ops:
  0.6 0.8 copy.28
  1.4 0.7 and_select_fusion
  2.1 0.1 iota_compare_fusion.1
  2.1 0.2 fusion.3
  2.4 1.1 copy.30
  3.5 0.8 copy.31.w_in_ref
  4.3 31.8 %project.1 = bf16[48,768]{1,0:T(8,128)(2,1)} custom-call(bf16[48,1024]{1,0:T(8,128)(2,1)} %tokens_ref.3, bf16[128,768]{1,0:T(8,128)(2,1)} %copy.31.w_in_ref), custom_call_target="tpu_custom_call" | custom-call | tf_op jit(solution)/shard_map/project/pallas_call | solution.py:135
  36.1 1.6 %fusion.13.query_ref = f32[160,256]{1,0:T(8,128)} fusion(pred[48,160]{1,0:T(8,128)(4,1)S(1)} %fusion.3, bf16[48,768]{1,0:T(8,128)(2,1)} %project.1), kind=kOutput, calls=%fused_computation.24 | convolution fusion | flops 3944448 | bytes 196096 | tf_op jit(solution)/shard_map/dot_general | solution.py:403
  37.7 0.8 clamp_select_fusion
  38.5 0.1 copy.29
  38.6 0.8 select_reduce_fusion.1.valid_ref
  39.4 0.0 copy-start.2
  39.4 0.0 copy-start
  39.4 0.0 copy-start.1
  39.4 22.8 %page_parts.1 = (f32[160,256]{1,0:T(8,128)}, f32[160,256]{1,0:T(8,128)}, f32[160,256]{1,0:T(8,128)}, bf16[8,256,128]{2,1,0:T(8,128)(2,1)}, bf16[1024,256]{1,0:T(8,128)(2,1)}) custom-call(s32[160]{0:T(256)} %select_reduce_fusion.1.valid_ref, f32[160,256]{1,0:T(8,128)} %fusion.13.query_ref, bf16[160,128,2,256]{3,2,1,0:T(2,128)(2,1)} %kv_ref.2, ...), custom_call_target="tpu_custom_call" | custom-call | flops 335544320 | bytes 20971520 | tf_op jit(solution)/shard_map/page_parts/pallas_call | solution.py:347
  62.2 0.0 copy-done.2
  62.2 3.6 %select_reduce_fusion = f32[48,256]{1,0:T(8,128)S(1)} fusion(f32[160,256]{1,0:T(8,128)} %get-tuple-element.12, pred[48,160]{1,0:T(8,128)(4,1)S(1)} %broadcast_and_fusion), kind=kLoop, calls=%fused_computation | loop fusion | flops 3919872 | bytes 220672 | tf_op jit(solution)/shard_map/reduce_max | solution.py:411
  65.9 0.0 copy-done
  65.9 0.1 reshape.147
  66.0 0.1 reduce_sum.19
  66.1 0.1 broadcast_in_dim.72
  66.3 0.1 reshape.148
  66.4 1.4 %fusion.20 = (f32[160,256]{1,0:T(8,128)S(1)}, f32[160,256]{1,0:T(8,128)S(1)}) fusion(f32[160,256]{1,0:T(8,128)} %get-tuple-element.11, f32[160,256]{1,0:T(8,128)} %get-tuple-element.13, f32[160,256]{1,0:T(8,128)} %get-tuple-element.12, pred[48,160]{1,0:T(8,128)(4,1)S(1)} %fusion.3, f32[48,256]{1,0:T(8,128)S(1)} %select_reduce_fusion, ...), kind=kOutput, calls=%fused_computation.47 | convolution fusion | flops 23769088 | bytes 925344 | tf_op jit(solution)/shard_map/dot_general | solution.py:413
  67.8 0.3 fusion.4
  68.0 0.6 fusion.11.ctx_ref
  68.7 1.9 %copy_bitcast_fusion.1.w_out_ref = bf16[256,1024]{1,0:T(8,128)(2,1)} fusion(bf16[8,256,128]{2,1,0:T(8,128)(2,1)} %get-tuple-element.14), kind=kLoop, calls=%fused_computation.5 | loop fusion | bytes 1048576 | tf_op jit(solution)/shard_map/reshape | solution.py:564
  70.6 15.7 %first_half.1 = (bf16[48,1024]{1,0:T(8,128)(2,1)}, bf16[384,256]{1,0:T(8,128)(2,1)}) custom-call(bf16[48,256]{1,0:T(8,128)(2,1)} %fusion.11.ctx_ref, bf16[48,1024]{1,0:T(8,128)(2,1)} %tokens_ref.3, bf16[256,1024]{1,0:T(8,128)(2,1)} %copy_bitcast_fusion.1.w_out_ref, bf16[1024,256]{1,0:T(8,128)(2,1)} %get-tuple-element.15.w_query_ref, f32[1,1024]{1,0:T(1,128)} %bitcast.39, ...), custom_call_target="tpu_custom_call" | custom-call | tf_op jit(solution)/shard_map/first_half/pallas_call | solution.py:223
  86.3 0.0 copy-done.1
  86.3 0.1 compare_convert_fusion
  86.4 1.2 reduce-window.6
  87.6 0.2 slice_reduce_fusion
  87.8 0.2 reduce-window.9
  88.0 0.1 add_bitcast_fusion
  88.1 0.1 broadcast_compare_fusion
  88.1 0.1 eq.75
  88.2 0.7 fusion.9.picker_ref
  88.9 16.0 %group_parts.1 = (bf16[384,256]{1,0:T(8,128)(2,1)}, bf16[8,256,128]{2,1,0:T(8,128)(2,1)}) custom-call(bf16[64,384]{1,0:T(8,128)(2,1)} %fusion.9.picker_ref, bf16[384,256]{1,0:T(8,128)(2,1)} %get-tuple-element.16.query_ref, bf16[4,2048,2,256]{3,2,1,0:T(2,128)(2,1)} %kv_ref.3, bf16[256,128]{1,0:T(8,128)(2,1)} %w_cross_ref.1), custom_call_target="tpu_custom_call" | custom-call | tf_op jit(solution)/shard_map/group_parts/pallas_call | solution.py:490
  104.9 1.9 %copy_bitcast_fusion.w_cross_ref = bf16[256,1024]{1,0:T(8,128)(2,1)} fusion(bf16[8,256,128]{2,1,0:T(8,128)(2,1)} %get-tuple-element.19), kind=kLoop, calls=%fused_computation.4 | loop fusion | bytes 1048576 | tf_op jit(solution)/shard_map/reshape | solution.py:571
  106.8 14.0 %last_half.1 = bf16[48,1024]{1,0:T(8,128)(2,1)} custom-call(bf16[384,256]{1,0:T(8,128)(2,1)} %get-tuple-element.17.placed_ref, bf16[48,1024]{1,0:T(8,128)(2,1)} %get-tuple-element.18.h_ref, bf16[256,1024]{1,0:T(8,128)(2,1)} %copy_bitcast_fusion.w_cross_ref, f32[1,1024]{1,0:T(1,128)} %bitcast.41, f32[1,1024]{1,0:T(1,128)} %bitcast.42), custom_call_target="tpu_custom_call" | custom-call | tf_op jit(solution)/shard_map/last_half/pallas_call | solution.py:243
  120.9 0.7 slice.35
  121.6 1.5 %copy.42 = bf16[48,1024]{1,0:T(8,128)(2,1)} copy(bf16[48,1024]{1,0:T(8,128)(2,1)} %last_half.1) | data formatting | bytes 196608
  (10 shorter events, 0.1 us)
Async XLA Ops:
  39.4 22.8 %copy-start.2 = (s32[160]{0:T(256)S(1)}, s32[160]{0:T(256)}, u32[]{:S(2)}) copy-start(s32[160]{0:T(256)} %select_reduce_fusion.1.valid_ref) | copy-start | bytes 1924
  39.4 26.5 %copy-start = (bf16[48,768]{1,0:T(8,128)(2,1)S(1)}, bf16[48,768]{1,0:T(8,128)(2,1)}, u32[]{:S(2)}) copy-start(bf16[48,768]{1,0:T(8,128)(2,1)} %project.1) | copy-start | bytes 221188
  39.4 46.9 %copy-start.1 = (s32[384]{0:T(512)S(1)}, s32[384]{0:T(512)}, u32[]{:S(2)}) copy-start(s32[384]{0:T(512)} %param.19) | copy-start | bytes 4612
